TPU v7x, 256 devices: a whole 4x4x8 slice. The times are simulated.
256 devices in a mesh: clus: 16 (over z, core), ang: 16 (over x, y).
Axes of the slice: x: 4, y: 4, z: 8, core: 2. Of those that a mesh axis runs over, the one named last changes fastest.
Arguments:
- child_pattern: float32 [512, 2, 128, 64], P('clus', None, 'ang'), may hold values from -6 to 6
- child_sources: int32 [512, 189], replicated, may hold values from 0 to 511
- child_classes: int32 [512, 189], replicated, may hold values from 0 to 315
- child_counts: int32 [512], replicated, may hold values from 1 to 189, as said below
- parent_sources: int32 [64, 189], replicated, may hold values from 0 to 63
- parent_classes: int32 [64, 189], replicated, may hold values from 0 to 315
- parent_counts: int32 [64], replicated, may hold values from 1 to 189, as said below
- child_table: float32 [316, 2, 128, 64], P(None, None, 'ang'), may hold values from -0.4375 to 0.4375
- parent_table: float32 [316, 2, 256, 128], P(None, None, 'ang'), may hold values from -0.15625 to 0.15625
- theta_index: int32 [128, 4], replicated, may hold values from 0 to 63, as said below
- theta_weight: float32 [128, 4], replicated, as said below
- phi_index: int32 [256, 4], P('ang'), may hold values from 0 to 127, as said below
- phi_weight: float32 [256, 4], P('ang'), as said below
- shift_angle: float32 [8, 256, 128], P(None, 'ang'), may hold values from -3.140625 to 3.140625
Outputs:
- child_incoming: float32 [512, 2, 128, 64], P('clus', None, 'ang')
- parent_pattern: float32 [64, 2, 256, 128], P('clus', None, 'ang')
- parent_incoming: float32 [64, 2, 256, 128], P('clus', None, 'ang')
Inputs may be any that keep to these rules, and one draw needn't show every extreme that they name: `child_counts`: the number of live slots of each child far list; slots beyond it are padding. `parent_counts`: the number of live slots of each parent far list; slots beyond it are padding. `theta_index`: row i holds four consecutive child rows beginning at min(max(i // 2 - 2 or i // 2 - 1, 0), 60). `phi_index`: row j holds four cyclically consecutive child columns beginning at j // 2 - 2 or j // 2 - 1, modulo 128. `theta_weight`: lagrange weights of four equispaced nodes. `phi_weight`: lagrange weights of four equispaced nodes.
All inputs are finite; a program needn't handle non-finite values.
Results may differ from a plain program's by a relative error of at most 0.00007.
Values sent between devices are 32-bit elements; how exact they have to be, the bound alone decides.
A program may use at most 64 MiB of HBM per device.

v0:
```python
import jax
import jax.numpy as jnp
from jax import lax
from jax.sharding import PartitionSpec as P


def extended(block, sides, width):
    for axis, dim in sides:
        count = lax.axis_size(axis)
        forward = [(i, i + 1) for i in range(count - 1)]
        forward.append((count - 1, 0))
        backward = [(target, source) for source, target in forward]
        low = lax.ppermute(
            lax.slice_in_dim(block, block.shape[dim] - width, None, axis=dim), axis, forward
        )
        high = lax.ppermute(lax.slice_in_dim(block, 0, width, axis=dim), axis, backward)
        block = jnp.concatenate([low, block, high], axis=dim)
    return block


def apply_lists(flat_pattern, source_ids, class_ids, live_counts, flat_table):
    dest_count, slot_count = source_ids.shape
    sample_count = flat_pattern.shape[2]
    pattern_rows = flat_pattern.reshape(flat_pattern.shape[0], 2 * sample_count)
    table_rows = flat_table.reshape(flat_table.shape[0], 2 * sample_count)
    blocks = 1
    while (
        dest_count % (blocks * 2) == 0
        and dest_count // blocks * slot_count * sample_count * 2 > 2**20
    ):
        blocks = blocks * 2

    def one_block(pieces):
        block_sources, block_classes, block_counts = pieces
        source_vals = pattern_rows[block_sources]
        factor = table_rows[block_classes]
        live = (jnp.arange(slot_count, dtype=jnp.int32)[None, :] < block_counts[:, None])[
            :, :, None
        ]
        source_real = source_vals[:, :, :sample_count]
        source_imag = source_vals[:, :, sample_count:]
        factor_real = factor[:, :, :sample_count]
        factor_imag = factor[:, :, sample_count:]
        real_part = source_real * factor_real - source_imag * factor_imag
        imag_part = source_real * factor_imag + source_imag * factor_real
        real_sum = jnp.sum(jnp.where(live, real_part, 0.0), axis=1)
        imag_sum = jnp.sum(jnp.where(live, imag_part, 0.0), axis=1)
        return jnp.concatenate([real_sum, imag_sum], axis=1)

    result = lax.map(
        one_block,
        (
            source_ids.reshape(blocks, -1, slot_count),
            class_ids.reshape(blocks, -1, slot_count),
            live_counts.reshape(blocks, -1),
        ),
    )
    return result.reshape(dest_count, 2, sample_count)


def stencil_matrix(index_table, weight_table, width):
    columns = jnp.arange(width, dtype=jnp.int32)
    hits = index_table[:, :, None] == columns[None, None, :]
    return jnp.sum(jnp.where(hits, weight_table[:, :, None], 0.0), axis=1)


def aggregate(child_pattern, theta_index, theta_weight, phi_index, phi_weight, shift_angle):
    haloed = extended(child_pattern, (("ang", 2),), 2)
    local_cols = child_pattern.shape[2]
    total_cols = local_cols * lax.axis_size("ang")
    first_col = lax.axis_index("ang") * local_cols
    offsets = (phi_index - first_col + 2) % total_cols
    phi_matrix = stencil_matrix(offsets, phi_weight, local_cols + 4)
    theta_matrix = stencil_matrix(theta_index, theta_weight, child_pattern.shape[3])
    polar = jnp.einsum("cqpt,it->cqpi", haloed, theta_matrix, precision=lax.Precision.HIGHEST)
    interpolated = jnp.einsum("cqpi,jp->cqji", polar, phi_matrix, precision=lax.Precision.HIGHEST)
    parent_count = child_pattern.shape[0] // 8
    grouped = interpolated.reshape((parent_count, 8) + interpolated.shape[1:])
    cosine = jnp.cos(shift_angle)[None]
    sine = jnp.sin(shift_angle)[None]
    real_part = jnp.sum(grouped[:, :, 0] * cosine - grouped[:, :, 1] * sine, axis=1)
    imag_part = jnp.sum(grouped[:, :, 0] * sine + grouped[:, :, 1] * cosine, axis=1)
    return jnp.stack([real_part, imag_part], 1)


def local(
    child_pattern,
    child_sources,
    child_classes,
    child_counts,
    parent_sources,
    parent_classes,
    parent_counts,
    child_table,
    parent_table,
    theta_index,
    theta_weight,
    phi_index,
    phi_weight,
    shift_angle,
):
    clus_rank = lax.axis_index("clus")
    own_children = child_pattern.shape[0]
    child_flat = child_pattern.reshape(own_children, 2, -1)
    child_tab = child_table.reshape(child_table.shape[0], 2, -1)
    parent_pattern = aggregate(
        child_pattern, theta_index, theta_weight, phi_index, phi_weight, shift_angle
    )
    own_parents = parent_pattern.shape[0]
    parent_flat = parent_pattern.reshape(own_parents, 2, -1)
    parent_tab = parent_table.reshape(parent_table.shape[0], 2, -1)
    all_children = lax.all_gather(child_flat, "clus", axis=0, tiled=True)
    child_first = clus_rank * own_children
    child_back = apply_lists(
        all_children,
        lax.dynamic_slice_in_dim(child_sources, child_first, own_children, 0),
        lax.dynamic_slice_in_dim(child_classes, child_first, own_children, 0),
        lax.dynamic_slice_in_dim(child_counts, child_first, own_children, 0),
        child_tab,
    )
    all_parents = lax.all_gather(parent_flat, "clus", axis=0, tiled=True)
    parent_first = clus_rank * own_parents
    parent_back = apply_lists(
        all_parents,
        lax.dynamic_slice_in_dim(parent_sources, parent_first, own_parents, 0),
        lax.dynamic_slice_in_dim(parent_classes, parent_first, own_parents, 0),
        lax.dynamic_slice_in_dim(parent_counts, parent_first, own_parents, 0),
        parent_tab,
    )
    child_incoming = child_back.reshape(child_pattern.shape)
    parent_incoming = parent_back.reshape(parent_pattern.shape)
    return (child_incoming, parent_pattern, parent_incoming)


def solution(mesh):
    return jax.shard_map(
        local,
        mesh=mesh,
        in_specs=(
            P("clus", None, "ang", None),
            P(),
            P(),
            P(),
            P(),
            P(),
            P(),
            P(None, None, "ang", None),
            P(None, None, "ang", None),
            P(),
            P(),
            P("ang", None),
            P("ang", None),
            P(None, "ang", None),
        ),
        out_specs=(
            P("clus", None, "ang", None),
            P("clus", None, "ang", None),
            P("clus", None, "ang", None),
        ),
        check_vma=False,
    )
```

profile of v0, /device:TPU:1, one launch (start us, length us, event | category | flops | bytes accessed | tf_op | source)
XLA Modules:
  0.0 298.0 jit_solution(11002513596476970264)
XLA Ops:
  8.3 5.8 %collective-permute-start.1 = (f32[32,2,2,64]{3,0,2,1:T(8,128)S(1)}, f32[32,2,2,64]{3,0,2,1:T(8,128)S(1)}, u32[]{:S(2)}, u32[]{:S(2)}) collective-permute-start(f32[32,2,2,64]{3,0,2,1:T(8,128)S(1)} %get-tuple-element.139), channel_id=1, source_target_pairs={{1,0},{2,1},{3,2},{4,3},{5,4},{6,5},{7,6},{8,7},{9,8},{10,9},{11,1... | collective-permute-start | bytes 98312 | tf_op jit(solution)/shard_map/ppermute | solution.py:16
  31.8 7.2 %copy.62 = f32[40,8,32,128]{3,1,2,0:T(8,128)} copy(f32[40,8,32,128]{3,2,1,0:T(8,128)S(1)} %bitcast.101) | data formatting | bytes 10485760
  39.6 22.1 %all-gather.5.cloned.1.call-done = f32[64,2,2048]{2,1,0:T(2,128)} async-done(((f32[4,2,2048]{2,1,0:T(2,128)}), f32[64,2,2048]{2,1,0:T(2,128)}) %all-gather.5.cloned.1.call-update) | async-done | bytes 1048592 | tf_op jit(solution)/shard_map/all_gather | solution.py:121
  63.5 61.5 %while.21 = (s32[]{:T(128)}, f32[4,1,4096]{2,1,0:T(1,128)S(1)}, s32[4,1]{0,1:T(1,128)S(1)}, s32[4,1,189]{2,1,0:T(1,128)S(1)}, f32[64,4096]{1,0:T(8,128)S(1)}, /*...) while((s32[]{:T(128)}, f32[4,1,4096]{2,1,0:T(1,128)S(1)}, s32[4,1]{0,1:T(1,128)S(1)}, ...), condition=%wide.region_11.12_spmd, body=%wide.region_8.11_spmd.sunk | while | flops 3874093 | bytes 18643344 | solution.py:50
  63.7 7.0 %gather_fusion.2 = f32[189,4096]{1,0:T(8,128)} fusion(f32[316,4096]{1,0:T(8,128)} %get-tuple-element.294, s32[1024]{0:T(1024)S(1)} %pad_clamp_fusion.10), kind=kCustom, calls=%fused_computation.3.clone.1 | custom fusion | bytes 6193908 | tf_op jit(solution)/shard_map/while/body/eval_jaxpr/gather | solution.py:36
  75.3 3.7 %select_reduce_fusion.9 = (f32[2048]{0:T(1024)S(1)}, f32[2048]{0:T(1024)S(1)}) fusion(f32[1,189,4096]{2,1,0:T(8,128)} %bitcast.99, f32[1,189,4096]{2,1,0:T(8,128)} %bitcast.100, pred[189]{0:T(512)(128)(4,1)S(1)} %iota_compare_fusion.7), kind=kLoop, calls=%fused_computation.16.clone.1 | loop fusion | flops 3866624 | bytes 6209725 | tf_op jit(solution)/shard_map/while/body/eval_jaxpr/reduce_sum | solution.py:46
  79.0 7.1 %gather_fusion.2 = f32[189,4096]{1,0:T(8,128)} fusion(f32[316,4096]{1,0:T(8,128)} %get-tuple-element.294, s32[1024]{0:T(1024)S(1)} %pad_clamp_fusion.10), kind=kCustom, calls=%fused_computation.3.clone.1 | custom fusion | bytes 6193908 | tf_op jit(solution)/shard_map/while/body/eval_jaxpr/gather | solution.py:36
  90.6 3.7 %select_reduce_fusion.9 = (f32[2048]{0:T(1024)S(1)}, f32[2048]{0:T(1024)S(1)}) fusion(f32[1,189,4096]{2,1,0:T(8,128)} %bitcast.99, f32[1,189,4096]{2,1,0:T(8,128)} %bitcast.100, pred[189]{0:T(512)(128)(4,1)S(1)} %iota_compare_fusion.7), kind=kLoop, calls=%fused_computation.16.clone.1 | loop fusion | flops 3866624 | bytes 6209725 | tf_op jit(solution)/shard_map/while/body/eval_jaxpr/reduce_sum | solution.py:46
  94.4 7.0 %gather_fusion.2 = f32[189,4096]{1,0:T(8,128)} fusion(f32[316,4096]{1,0:T(8,128)} %get-tuple-element.294, s32[1024]{0:T(1024)S(1)} %pad_clamp_fusion.10), kind=kCustom, calls=%fused_computation.3.clone.1 | custom fusion | bytes 6193908 | tf_op jit(solution)/shard_map/while/body/eval_jaxpr/gather | solution.py:36
  106.0 3.7 %select_reduce_fusion.9 = (f32[2048]{0:T(1024)S(1)}, f32[2048]{0:T(1024)S(1)}) fusion(f32[1,189,4096]{2,1,0:T(8,128)} %bitcast.99, f32[1,189,4096]{2,1,0:T(8,128)} %bitcast.100, pred[189]{0:T(512)(128)(4,1)S(1)} %iota_compare_fusion.7), kind=kLoop, calls=%fused_computation.16.clone.1 | loop fusion | flops 3866624 | bytes 6209725 | tf_op jit(solution)/shard_map/while/body/eval_jaxpr/reduce_sum | solution.py:46
  109.7 7.0 %gather_fusion.2 = f32[189,4096]{1,0:T(8,128)} fusion(f32[316,4096]{1,0:T(8,128)} %get-tuple-element.294, s32[1024]{0:T(1024)S(1)} %pad_clamp_fusion.10), kind=kCustom, calls=%fused_computation.3.clone.1 | custom fusion | bytes 6193908 | tf_op jit(solution)/shard_map/while/body/eval_jaxpr/gather | solution.py:36
  121.3 3.7 %select_reduce_fusion.9 = (f32[2048]{0:T(1024)S(1)}, f32[2048]{0:T(1024)S(1)}) fusion(f32[1,189,4096]{2,1,0:T(8,128)} %bitcast.99, f32[1,189,4096]{2,1,0:T(8,128)} %bitcast.100, pred[189]{0:T(512)(128)(4,1)S(1)} %iota_compare_fusion.7), kind=kLoop, calls=%fused_computation.16.clone.1 | loop fusion | flops 3866624 | bytes 6209725 | tf_op jit(solution)/shard_map/while/body/eval_jaxpr/reduce_sum | solution.py:46
  127.7 162.6 %while.20 = (s32[]{:T(128)}, f32[8,4,1024]{2,1,0:T(4,128)S(1)}, s32[8,4]{1,0:T(8,128)}, s32[8,4,189]{2,1,0:T(4,128)}, f32[512,1024]{1,0:T(8,128)S(1)}, /*index=5...) while((s32[]{:T(128)}, f32[8,4,1024]{2,1,0:T(4,128)S(1)}, s32[8,4]{1,0:T(8,128)}, ...), condition=%wide.region_3.4_spmd, body=%wide.region_0.3_spmd.sunk | while | flops 3878062 | bytes 31061056 | solution.py:50
  128.5 3.6 %gather_fusion = f32[756,1024]{1,0:T(8,128)} fusion(f32[316,1024]{1,0:T(8,128)S(1)} %get-tuple-element.270, s32[1024]{0:T(1024)S(1)} %pad_clamp_fusion.8), kind=kCustom, calls=%fused_computation.1.clone.1 | custom fusion | bytes 6196176 | tf_op jit(solution)/shard_map/while/body/eval_jaxpr/gather | solution.py:36
  132.2 3.9 %reshape.281 = f32[4,189,1024]{2,1,0:T(8,128)} reshape(f32[756,1024]{1,0:T(8,128)} %gather_fusion) | data formatting | bytes 6193152 | tf_op jit(solution)/shard_map/while/body/eval_jaxpr/gather | solution.py:36
  136.2 3.7 %gather_fusion.1 = f32[756,1024]{1,0:T(8,128)} fusion(f32[512,1024]{1,0:T(8,128)S(1)} %get-tuple-element.268, s32[1024]{0:T(1024)S(1)} %pad_clamp_fusion.9), kind=kCustom, calls=%fused_computation.clone.1 | custom fusion | bytes 6196176 | tf_op jit(solution)/shard_map/while/body/eval_jaxpr/gather | solution.py:35
  139.9 3.9 %reshape.283 = f32[4,189,1024]{2,1,0:T(8,128)} reshape(f32[756,1024]{1,0:T(8,128)} %gather_fusion.1) | data formatting | bytes 6193152 | tf_op jit(solution)/shard_map/while/body/eval_jaxpr/gather | solution.py:35
  144.6 3.4 %select_reduce_fusion.8 = (f32[4,512]{1,0:T(4,128)S(1)}, f32[4,512]{1,0:T(4,128)S(1)}) fusion(f32[4,189,1024]{2,1,0:T(8,128)} %reshape.281, f32[4,189,1024]{2,1,0:T(8,128)} %reshape.283, pred[4,189]{1,0:T(4,128)(4,1)S(1)} %iota_compare_fusion.6), kind=kLoop, calls=%fused_computation.5.clone.1 | loop fusion | flops 3866624 | bytes 6210292 | tf_op jit(solution)/shard_map/while/body/eval_jaxpr/reduce_sum | solution.py:46
  148.8 3.6 %gather_fusion = f32[756,1024]{1,0:T(8,128)} fusion(f32[316,1024]{1,0:T(8,128)S(1)} %get-tuple-element.270, s32[1024]{0:T(1024)S(1)} %pad_clamp_fusion.8), kind=kCustom, calls=%fused_computation.1.clone.1 | custom fusion | bytes 6196176 | tf_op jit(solution)/shard_map/while/body/eval_jaxpr/gather | solution.py:36
  152.5 3.9 %reshape.281 = f32[4,189,1024]{2,1,0:T(8,128)} reshape(f32[756,1024]{1,0:T(8,128)} %gather_fusion) | data formatting | bytes 6193152 | tf_op jit(solution)/shard_map/while/body/eval_jaxpr/gather | solution.py:36
  156.5 3.7 %gather_fusion.1 = f32[756,1024]{1,0:T(8,128)} fusion(f32[512,1024]{1,0:T(8,128)S(1)} %get-tuple-element.268, s32[1024]{0:T(1024)S(1)} %pad_clamp_fusion.9), kind=kCustom, calls=%fused_computation.clone.1 | custom fusion | bytes 6196176 | tf_op jit(solution)/shard_map/while/body/eval_jaxpr/gather | solution.py:35
  160.2 3.9 %reshape.283 = f32[4,189,1024]{2,1,0:T(8,128)} reshape(f32[756,1024]{1,0:T(8,128)} %gather_fusion.1) | data formatting | bytes 6193152 | tf_op jit(solution)/shard_map/while/body/eval_jaxpr/gather | solution.py:35
  169.2 3.6 %gather_fusion = f32[756,1024]{1,0:T(8,128)} fusion(f32[316,1024]{1,0:T(8,128)S(1)} %get-tuple-element.270, s32[1024]{0:T(1024)S(1)} %pad_clamp_fusion.8), kind=kCustom, calls=%fused_computation.1.clone.1 | custom fusion | bytes 6196176 | tf_op jit(solution)/shard_map/while/body/eval_jaxpr/gather | solution.py:36
  172.8 3.9 %reshape.281 = f32[4,189,1024]{2,1,0:T(8,128)} reshape(f32[756,1024]{1,0:T(8,128)} %gather_fusion) | data formatting | bytes 6193152 | tf_op jit(solution)/shard_map/while/body/eval_jaxpr/gather | solution.py:36
  176.8 3.7 %gather_fusion.1 = f32[756,1024]{1,0:T(8,128)} fusion(f32[512,1024]{1,0:T(8,128)S(1)} %get-tuple-element.268, s32[1024]{0:T(1024)S(1)} %pad_clamp_fusion.9), kind=kCustom, calls=%fused_computation.clone.1 | custom fusion | bytes 6196176 | tf_op jit(solution)/shard_map/while/body/eval_jaxpr/gather | solution.py:35
  180.5 3.9 %reshape.283 = f32[4,189,1024]{2,1,0:T(8,128)} reshape(f32[756,1024]{1,0:T(8,128)} %gather_fusion.1) | data formatting | bytes 6193152 | tf_op jit(solution)/shard_map/while/body/eval_jaxpr/gather | solution.py:35
  185.2 3.4 %select_reduce_fusion.8 = (f32[4,512]{1,0:T(4,128)S(1)}, f32[4,512]{1,0:T(4,128)S(1)}) fusion(f32[4,189,1024]{2,1,0:T(8,128)} %reshape.281, f32[4,189,1024]{2,1,0:T(8,128)} %reshape.283, pred[4,189]{1,0:T(4,128)(4,1)S(1)} %iota_compare_fusion.6), kind=kLoop, calls=%fused_computation.5.clone.1 | loop fusion | flops 3866624 | bytes 6210292 | tf_op jit(solution)/shard_map/while/body/eval_jaxpr/reduce_sum | solution.py:46
  189.5 3.6 %gather_fusion = f32[756,1024]{1,0:T(8,128)} fusion(f32[316,1024]{1,0:T(8,128)S(1)} %get-tuple-element.270, s32[1024]{0:T(1024)S(1)} %pad_clamp_fusion.8), kind=kCustom, calls=%fused_computation.1.clone.1 | custom fusion | bytes 6196176 | tf_op jit(solution)/shard_map/while/body/eval_jaxpr/gather | solution.py:36
  193.1 3.9 %reshape.281 = f32[4,189,1024]{2,1,0:T(8,128)} reshape(f32[756,1024]{1,0:T(8,128)} %gather_fusion) | data formatting | bytes 6193152 | tf_op jit(solution)/shard_map/while/body/eval_jaxpr/gather | solution.py:36
  197.1 3.7 %gather_fusion.1 = f32[756,1024]{1,0:T(8,128)} fusion(f32[512,1024]{1,0:T(8,128)S(1)} %get-tuple-element.268, s32[1024]{0:T(1024)S(1)} %pad_clamp_fusion.9), kind=kCustom, calls=%fused_computation.clone.1 | custom fusion | bytes 6196176 | tf_op jit(solution)/shard_map/while/body/eval_jaxpr/gather | solution.py:35
  200.8 3.9 %reshape.283 = f32[4,189,1024]{2,1,0:T(8,128)} reshape(f32[756,1024]{1,0:T(8,128)} %gather_fusion.1) | data formatting | bytes 6193152 | tf_op jit(solution)/shard_map/while/body/eval_jaxpr/gather | solution.py:35
  205.5 3.4 %select_reduce_fusion.8 = (f32[4,512]{1,0:T(4,128)S(1)}, f32[4,512]{1,0:T(4,128)S(1)}) fusion(f32[4,189,1024]{2,1,0:T(8,128)} %reshape.281, f32[4,189,1024]{2,1,0:T(8,128)} %reshape.283, pred[4,189]{1,0:T(4,128)(4,1)S(1)} %iota_compare_fusion.6), kind=kLoop, calls=%fused_computation.5.clone.1 | loop fusion | flops 3866624 | bytes 6210292 | tf_op jit(solution)/shard_map/while/body/eval_jaxpr/reduce_sum | solution.py:46
  209.8 3.6 %gather_fusion = f32[756,1024]{1,0:T(8,128)} fusion(f32[316,1024]{1,0:T(8,128)S(1)} %get-tuple-element.270, s32[1024]{0:T(1024)S(1)} %pad_clamp_fusion.8), kind=kCustom, calls=%fused_computation.1.clone.1 | custom fusion | bytes 6196176 | tf_op jit(solution)/shard_map/while/body/eval_jaxpr/gather | solution.py:36
  213.5 3.9 %reshape.281 = f32[4,189,1024]{2,1,0:T(8,128)} reshape(f32[756,1024]{1,0:T(8,128)} %gather_fusion) | data formatting | bytes 6193152 | tf_op jit(solution)/shard_map/while/body/eval_jaxpr/gather | solution.py:36
  217.4 3.7 %gather_fusion.1 = f32[756,1024]{1,0:T(8,128)} fusion(f32[512,1024]{1,0:T(8,128)S(1)} %get-tuple-element.268, s32[1024]{0:T(1024)S(1)} %pad_clamp_fusion.9), kind=kCustom, calls=%fused_computation.clone.1 | custom fusion | bytes 6196176 | tf_op jit(solution)/shard_map/while/body/eval_jaxpr/gather | solution.py:35
  221.2 3.9 %reshape.283 = f32[4,189,1024]{2,1,0:T(8,128)} reshape(f32[756,1024]{1,0:T(8,128)} %gather_fusion.1) | data formatting | bytes 6193152 | tf_op jit(solution)/shard_map/while/body/eval_jaxpr/gather | solution.py:35
  230.1 3.6 %gather_fusion = f32[756,1024]{1,0:T(8,128)} fusion(f32[316,1024]{1,0:T(8,128)S(1)} %get-tuple-element.270, s32[1024]{0:T(1024)S(1)} %pad_clamp_fusion.8), kind=kCustom, calls=%fused_computation.1.clone.1 | custom fusion | bytes 6196176 | tf_op jit(solution)/shard_map/while/body/eval_jaxpr/gather | solution.py:36
  233.8 3.9 %reshape.281 = f32[4,189,1024]{2,1,0:T(8,128)} reshape(f32[756,1024]{1,0:T(8,128)} %gather_fusion) | data formatting | bytes 6193152 | tf_op jit(solution)/shard_map/while/body/eval_jaxpr/gather | solution.py:36
  237.8 3.7 %gather_fusion.1 = f32[756,1024]{1,0:T(8,128)} fusion(f32[512,1024]{1,0:T(8,128)S(1)} %get-tuple-element.268, s32[1024]{0:T(1024)S(1)} %pad_clamp_fusion.9), kind=kCustom, calls=%fused_computation.clone.1 | custom fusion | bytes 6196176 | tf_op jit(solution)/shard_map/while/body/eval_jaxpr/gather | solution.py:35
  241.5 3.9 %reshape.283 = f32[4,189,1024]{2,1,0:T(8,128)} reshape(f32[756,1024]{1,0:T(8,128)} %gather_fusion.1) | data formatting | bytes 6193152 | tf_op jit(solution)/shard_map/while/body/eval_jaxpr/gather | solution.py:35
  250.5 3.6 %gather_fusion = f32[756,1024]{1,0:T(8,128)} fusion(f32[316,1024]{1,0:T(8,128)S(1)} %get-tuple-element.270, s32[1024]{0:T(1024)S(1)} %pad_clamp_fusion.8), kind=kCustom, calls=%fused_computation.1.clone.1 | custom fusion | bytes 6196176 | tf_op jit(solution)/shard_map/while/body/eval_jaxpr/gather | solution.py:36
  254.1 3.9 %reshape.281 = f32[4,189,1024]{2,1,0:T(8,128)} reshape(f32[756,1024]{1,0:T(8,128)} %gather_fusion) | data formatting | bytes 6193152 | tf_op jit(solution)/shard_map/while/body/eval_jaxpr/gather | solution.py:36
  258.1 3.7 %gather_fusion.1 = f32[756,1024]{1,0:T(8,128)} fusion(f32[512,1024]{1,0:T(8,128)S(1)} %get-tuple-element.268, s32[1024]{0:T(1024)S(1)} %pad_clamp_fusion.9), kind=kCustom, calls=%fused_computation.clone.1 | custom fusion | bytes 6196176 | tf_op jit(solution)/shard_map/while/body/eval_jaxpr/gather | solution.py:35
  261.8 3.9 %reshape.283 = f32[4,189,1024]{2,1,0:T(8,128)} reshape(f32[756,1024]{1,0:T(8,128)} %gather_fusion.1) | data formatting | bytes 6193152 | tf_op jit(solution)/shard_map/while/body/eval_jaxpr/gather | solution.py:35
  270.8 3.6 %gather_fusion = f32[756,1024]{1,0:T(8,128)} fusion(f32[316,1024]{1,0:T(8,128)S(1)} %get-tuple-element.270, s32[1024]{0:T(1024)S(1)} %pad_clamp_fusion.8), kind=kCustom, calls=%fused_computation.1.clone.1 | custom fusion | bytes 6196176 | tf_op jit(solution)/shard_map/while/body/eval_jaxpr/gather | solution.py:36
  274.4 3.9 %reshape.281 = f32[4,189,1024]{2,1,0:T(8,128)} reshape(f32[756,1024]{1,0:T(8,128)} %gather_fusion) | data formatting | bytes 6193152 | tf_op jit(solution)/shard_map/while/body/eval_jaxpr/gather | solution.py:36
  278.4 3.7 %gather_fusion.1 = f32[756,1024]{1,0:T(8,128)} fusion(f32[512,1024]{1,0:T(8,128)S(1)} %get-tuple-element.268, s32[1024]{0:T(1024)S(1)} %pad_clamp_fusion.9), kind=kCustom, calls=%fused_computation.clone.1 | custom fusion | bytes 6196176 | tf_op jit(solution)/shard_map/while/body/eval_jaxpr/gather | solution.py:35
  282.2 3.9 %reshape.283 = f32[4,189,1024]{2,1,0:T(8,128)} reshape(f32[756,1024]{1,0:T(8,128)} %gather_fusion.1) | data formatting | bytes 6193152 | tf_op jit(solution)/shard_map/while/body/eval_jaxpr/gather | solution.py:35
  (143 shorter events, 73.3 us)
Async XLA Ops:
  7.2 20.7 %copy-start = (s32[64]{0:T(128)S(1)}, s32[64]{0:T(128)}, u32[]{:S(2)}) copy-start(s32[64]{0:T(128)} %param.24) | copy-start | bytes 772
  7.2 15.5 %copy-start.2 = (f32[32,2,8,64]{3,2,1,0:T(8,128)S(1)}, f32[32,2,8,64]{3,2,1,0:T(8,128)}, u32[]{:S(2)}) copy-start(f32[32,2,8,64]{3,2,1,0:T(8,128)} %param.18) | copy-start | bytes 393220
  7.2 54.5 %all-gather.5.cloned.1.call-start = ((), (), s32[]{:S(2)}) async-start(), calls=%async_computation.1 | async-start | bytes 1114112 | tf_op jit(solution)/shard_map/all_gather | solution.py:121
  8.3 9.2 %collective-permute-start.1 = (f32[32,2,2,64]{3,0,2,1:T(8,128)S(1)}, f32[32,2,2,64]{3,0,2,1:T(8,128)S(1)}, u32[]{:S(2)}, u32[]{:S(2)}) collective-permute-start(f32[32,2,2,64]{3,0,2,1:T(8,128)S(1)} %get-tuple-element.139), channel_id=1, source_target_pairs={{1,0},{2,1},{3,2},{4,3},{5,4},{6,5},{7,6},{8,7},{9,8},{10,9},{11,1... | collective-permute-start | bytes 98312 | tf_op jit(solution)/shard_map/ppermute | solution.py:16
  14.2 6.4 %collective-permute-start = (f32[32,2,2,64]{3,0,2,1:T(8,128)S(1)}, f32[32,2,2,64]{3,0,2,1:T(8,128)S(1)}, u32[]{:S(2)}, u32[]{:S(2)}) collective-permute-start(f32[32,2,2,64]{3,0,2,1:T(8,128)S(1)} %get-tuple-element.138), channel_id=1, source_target_pairs={{0,1},{1,2},{2,3},{3,4},{4,5},{5,6},{6,7},{7,8},{8,9},{9,10},{10,1... | collective-permute-start | bytes 98312 | tf_op jit(solution)/shard_map/ppermute | solution.py:13
  16.0 11.5 %copy-start.1 = (f32[316,2,8,64]{0,3,2,1:T(8,128)S(1)}, f32[316,2,8,64]{0,3,2,1:T(8,128)}, u32[]{:S(2)}) copy-start(f32[316,2,8,64]{0,3,2,1:T(8,128)} %param.25) | copy-start | bytes 3883012
  22.6 102.4 %all-gather.3.cloned.1.call-start = ((), (), s32[]{:S(2)}) async-start(), calls=%async_computation | async-start | bytes 2228224 | tf_op jit(solution)/shard_map/all_gather | solution.py:112
  125.0 0.6 copy-start.3
Sparse Core Ops, SparseCore 0:
  22.8 38.8 all-gather.4
  64.0 38.4 all-gather.2
where the time goes:
time: 300 us; the launch traced here: 298 us
  local copies, waits for them, and re-layouts  196 us (65%)
  other arithmetic  55.1 us (18%)
  waiting for transfers between devices  25.2 us (8%)
  between operations  14.2 us (5%)
  starting transfers between devices  5.92 us (2%)
    gather x20, local copies, waits for them, and re-layouts, one_block(): factor = table_rows[block_classes]  88.5 us
    gather x20, local copies, waits for them, and re-layouts, one_block(): source_vals = pattern_rows[block_sources]  74.5 us
    reduce_sum x12, other arithmetic, one_block(): real_sum = jnp.sum(jnp.where(live, real_part, 0.0), axis=1)  42.2 us
    all_gather x1, waiting for transfers between devices, local(): all_parents = lax.all_gather(parent_flat, 'clus', axis=0, tiled=True)  22.1 us
    unnamed x13, local copies, waits for them, and re-layouts  15.8 us
  transfers between devices with their start and end apart: 4, of which 2 were waited for; matrix products, arithmetic and copies ran while one was open for 28% of the time, Pallas kernels for 0%

commit v1 on v0

v1 whole, which is shorter than its diff:
```python
import functools

import jax
import jax.numpy as jnp
from jax import lax
from jax.experimental import pallas as pl
from jax.experimental.pallas import tpu as pltpu
from jax.sharding import PartitionSpec as P

MESH = pl.DeviceIdType.MESH
SLOTS = 189
CLASSES = 316
HEAD = 96
TAIL = 32
CHUNKS = 2
CHILD_STEPS = -(-(SLOTS - HEAD) // TAIL)
PARENT_STEPS = -(-SLOTS // TAIL)
CHILD_ROWS = 32 * CHILD_STEPS
PARENT_ROWS = 8 * PARENT_STEPS


def rows_at(start, size):
    return pl.ds(pl.multiple_of(start, 8), size)


def gather_kernel(
    pat_hbm, cs_hbm, cc_hbm, ccnt_hbm, ps_hbm, pc_hbm, pcnt_hbm, tab_hbm,
    thi_hbm, thw_hbm, phi_hbm, phw_hbm, ang_hbm,
    g_ref, f_ref, acc_ref, pg_ref, ci_ref, pi_ref,
    pat, sv, cv, ccnt, psv, pcv, pcnt, tab, thi, thw, phi, phw, ang,
    own, hs, hr, zs, ta, sa_s, sa_c,
    loc, smsem, hsend, hrecv, csend, crecv, cssend, csrecv, psend, precv, pssend, psrecv,
):
    r = lax.axis_index("clus")
    a = lax.axis_index("ang")
    sib = r + 1 - 2 * lax.rem(r, 2)
    up, down = lax.rem(r + 2, 16), lax.rem(r + 14, 16)
    ahead, behind = lax.rem(a + 1, 16), lax.rem(a + 15, 16)

    lane_block = pl.ds(pl.multiple_of(lax.div(r, 4) * 128, 128), 128)
    row_block = rows_at(lax.div(r, 2) * 8, 8)
    locals_ = [
        (pat_hbm, pat),
        (cs_hbm.at[:, lane_block], sv),
        (cc_hbm.at[:, lane_block], cv),
        (ccnt_hbm, ccnt),
        (ps_hbm.at[row_block, :], psv),
        (pc_hbm.at[row_block, :], pcv),
        (pcnt_hbm, pcnt),
        (thi_hbm, thi),
        (thw_hbm, thw),
        (phi_hbm, phi),
        (phw_hbm, phw),
        (ang_hbm, ang),
        (tab_hbm, tab),
    ]
    copies = [pltpu.make_async_copy(src, dst, loc.at[i]) for i, (src, dst) in enumerate(locals_)]
    for copy in copies:
        copy.start()

    barrier = pltpu.get_barrier_semaphore()
    for target in (up, down, sib):
        pl.semaphore_signal(barrier, inc=1, device_id={"clus": target}, device_id_type=MESH)
    for target in (ahead, behind):
        pl.semaphore_signal(barrier, inc=1, device_id={"ang": target}, device_id_type=MESH)
    pl.semaphore_wait(barrier, 5)

    def mover(buffer, block_rows, send, recv, sib_send, sib_recv):
        size = block_rows // CHUNKS

        def part(owner, ch):
            return buffer.at[rows_at(owner * block_rows + ch * size, size), :]

        def ring(way, step, ch):
            back = 16 - 2 * (step - 1) if way == 0 else 2 * (step - 1)
            block = part(lax.rem(r + back, 16), ch)
            k = (8 - step) if way == 0 else step
            return pltpu.make_async_remote_copy(
                src_ref=block, dst_ref=block,
                send_sem=send.at[way, step - 1, ch], recv_sem=recv.at[k, ch],
                device_id={"clus": up if way == 0 else down}, device_id_type=MESH,
            )

        def arrived(way, step, ch):
            k = (8 - step) if way == 0 else step
            block = part(lax.rem(r + 2 * k, 16), ch)
            pltpu.make_async_remote_copy(
                src_ref=block, dst_ref=block,
                send_sem=send.at[way, step - 1, ch], recv_sem=recv.at[k, ch],
                device_id={"clus": up if way == 0 else down}, device_id_type=MESH,
            ).wait_recv()

        def side(k, ch, mine=True):
            block = part(lax.rem((r if mine else sib) + 2 * k, 16), ch)
            return pltpu.make_async_remote_copy(
                src_ref=block, dst_ref=block,
                send_sem=sib_send.at[k, ch], recv_sem=sib_recv.at[k, ch],
                device_id={"clus": sib}, device_id_type=MESH,
            )

        def uses(way, step, ch):
            return step < 4 or (ch < CHUNKS // 2) == (way == 0)

        def first(ch):
            for way in (0, 1):
                ring(way, 1, ch).start()
            side(0, ch).start()

        def onward(step, ch):
            for way in (0, 1):
                if uses(way, step, ch):
                    arrived(way, step, ch)
                    if step < 4 and uses(way, step + 1, ch):
                        ring(way, step + 1, ch).start()
                    side((8 - step) if way == 0 else step, ch).start()

        def landed():
            for k in range(8):
                for ch in range(CHUNKS):
                    side(k, ch, mine=False).wait_recv()

        def drained():
            for ch in range(CHUNKS):
                for step in range(1, 5):
                    for way in (0, 1):
                        if uses(way, step, ch):
                            ring(way, step, ch).wait_send()
                for k in range(8):
                    side(k, ch).wait_send()

        return first, onward, landed, drained

    c_first, c_onward, c_landed, c_drained = mover(g_ref, 256, csend, crecv, cssend, csrecv)
    p_first, p_onward, p_landed, p_drained = mover(pg_ref, 128, psend, precv, pssend, psrecv)

    copies[0].wait()
    size = 32 // CHUNKS
    for ch in range(CHUNKS):
        x = pat[ch * size:(ch + 1) * size]
        x = jnp.concatenate([x[:, 0], x[:, 1]], axis=2).reshape(size * 8, 128)
        own[ch * size * 8:(ch + 1) * size * 8, :] = x
        g_ref[rows_at(r * 256 + ch * size * 8, size * 8), :] = x
        c_first(ch)

    halo = []
    for way in (0, 1):
        for j in range(2):
            hs[way, j * 32:(j + 1) * 32, :] = own[pl.ds((6 if way == 0 else 0) + j, 32, stride=8), :]
        copy = pltpu.make_async_remote_copy(
            src_ref=hs.at[way], dst_ref=hr.at[way], send_sem=hsend.at[way], recv_sem=hrecv.at[way],
            device_id={"ang": ahead if way == 0 else behind}, device_id_type=MESH,
        )
        copy.start()
        halo.append(copy)

    for i in (1, 2, 3):
        copies[i].wait()
    count_row = ccnt[pl.ds(lax.div(r, 4), 1), :]
    own_rows = rows_at(lax.rem(r, 4) * 32, 32)
    slot = lax.broadcasted_iota(jnp.int32, (128, 128), 0)

    def lists(start, stop):
        s, c = sv[start:stop, :], cv[start:stop, :]
        live = slot[:stop - start] + start < count_row
        s = jnp.where(live, s, 0) * 8
        c = jnp.where(live, c, CLASSES) * 16
        return s, c

    s, c = lists(0, 128)
    ta[0] = lax.shift_right_logical(s, 3).T
    ta[1] = lax.shift_right_logical(c, 4).T
    fill = [
        pltpu.make_async_copy(ta.at[0, own_rows, :], sa_s, smsem.at[0]),
        pltpu.make_async_copy(ta.at[1, own_rows, :], sa_c, smsem.at[1]),
    ]
    for copy in fill:
        copy.start()

    c_onward(1, 0)

    s, c = lists(HEAD, SLOTS)
    rest = 128 - (SLOTS - HEAD)
    s = jnp.concatenate([s, jnp.zeros((rest, 128), jnp.int32)], axis=0)
    c = jnp.concatenate([c, jnp.full((rest, 128), CLASSES * 16, jnp.int32)], axis=0)
    c = jnp.where(slot == 127, count_row, c)
    ta[2] = s.T
    ta[3] = c.T
    ts, tc = ta[2, own_rows, :], ta[3, own_rows, :]
    for i in range(CHILD_STEPS):
        ci_ref[i * 32:(i + 1) * 32, :] = pltpu.roll(ts, (128 - i * TAIL) % 128, 1) if i else ts
        ci_ref[CHILD_ROWS + i * 32:CHILD_ROWS + (i + 1) * 32, :] = (
            pltpu.roll(tc, (128 - i * TAIL) % 128, 1) if i else tc
        )

    for i in (4, 5, 6):
        copies[i].wait()
    line = lax.broadcasted_iota(jnp.int32, (8, 128), 0)
    lane = lax.broadcasted_iota(jnp.int32, (8, 128), 1)
    counts = jnp.zeros((8, 128), jnp.int32)
    for i in range(8):
        counts = jnp.where(line == i, pcnt[lax.div(r, 2) * 8 + i], counts)
    pads = jnp.zeros((8, 256 - SLOTS), jnp.int32)
    for half in range(2):
        if half == 0:
            s, c = psv[:, :128], pcv[:, :128]
        else:
            s = jnp.concatenate([psv[:, 128:], pads], axis=1)
            c = jnp.concatenate([pcv[:, 128:], pads], axis=1)
        live = lane + half * 128 < counts
        s = jnp.where(live, s, 64) * 32
        c = jnp.where(live, c, 0) * 32
        for i in range(half * 128 // TAIL, min((half + 1) * 128 // TAIL, PARENT_STEPS)):
            turn = (128 - (i * TAIL - half * 128)) % 128
            si = pltpu.roll(s, turn, 1) if turn else s
            cj = pltpu.roll(c, turn, 1) if turn else c
            pi_ref[i * 8:(i + 1) * 8, :] = si
            pi_ref[PARENT_ROWS + i * 8:PARENT_ROWS + (i + 1) * 8, :] = jnp.where(lane == 127, counts, cj)
    pg_ref[2048:2080, :] = jnp.zeros((32, 128), jnp.float32)

    c_onward(1, 1)

    copies[12].wait()

    def operators(col):
        for b in range(3):
            lo, hi = b * 128, min((b + 1) * 128, CLASSES)
            x = jnp.concatenate([tab[0, col, :, lo:hi], tab[1, col, :, lo:hi]], axis=0)
            if hi - lo < 128:
                x = jnp.concatenate([x, jnp.zeros((128, 128 - (hi - lo)), jnp.float32)], axis=1)
            y = x.T
            f_ref[pl.ds(lo * 16 + col, 128, stride=16), :] = y
            f_ref[pl.ds(lo * 16 + col + 8, 128, stride=16), :] = pltpu.roll(y, 64, 1)

    for col in range(4):
        operators(col)
    c_onward(2, 0)
    for col in range(4, 8):
        operators(col)
    c_onward(2, 1)

    for i in (7, 8, 9, 10, 11):
        copies[i].wait()
    for copy in halo:
        copy.wait_recv()
    offset = lax.rem(phi[...] - a * 8 + (2 + 128), 128)
    weights = phw[...]
    base = lax.shift_right_logical(lax.broadcasted_iota(jnp.int32, (1, 16), 1), 1)
    taps = []
    for d in range(5):
        tap = jnp.zeros((1, 16), jnp.float32)
        for i in range(4):
            tap = tap + jnp.where(offset[i:i + 1, :] == base + d, weights[i:i + 1, :], 0.0)
        taps.append(tap)
    cols = [hr[0, :32, :], hr[0, 32:, :]]
    cols += [own[pl.ds(j, 32, stride=8), :] for j in range(8)]
    cols += [hr[1, :32, :], hr[1, 32:, :]]
    for j in range(16):
        z = jnp.zeros((32, 128), jnp.float32)
        for d in range(5):
            z = z + taps[d][:, j:j + 1] * cols[j // 2 + d]
        zs[pl.ds(j, 32, stride=16), :] = z

    c_onward(3, 0)

    row = lax.broadcasted_iota(jnp.int32, (64, 128), 0)
    theta = jnp.zeros((64, 128), jnp.float32)
    for i in range(4):
        theta = theta + jnp.where(thi[i:i + 1, :] == row, thw[i:i + 1, :], 0.0)
    blank = jnp.zeros((64, 128), jnp.float32)
    pair = jnp.concatenate(
        [jnp.concatenate([theta, blank], axis=1), jnp.concatenate([blank, theta], axis=1)], axis=0
    )
    angles = ang[...]
    cosine, sine = jnp.cos(angles), jnp.sin(angles)

    c_onward(3, 1)

    for parent in range(4):
        y = jnp.dot(
            zs[parent * 128:(parent + 1) * 128, :], pair,
            precision=lax.Precision.HIGHEST, preferred_element_type=jnp.float32,
        )
        re = y[:, :128] * cosine - y[:, 128:] * sine
        im = y[:, :128] * sine + y[:, 128:] * cosine
        re = jnp.sum(re.reshape(8, 16, 128), axis=0)
        im = jnp.sum(im.reshape(8, 16, 128), axis=0)
        pg_ref[rows_at(r * 128 + parent * 32, 16), :] = re
        pg_ref[rows_at(r * 128 + parent * 32 + 16, 16), :] = im
        if parent % 2:
            p_first(parent // 2)

    for ch in range(CHUNKS):
        c_onward(4, ch)
    for copy in fill:
        copy.wait()
    c_landed()

    events = {}
    for i, (step, ch) in enumerate([(s, h) for s in range(1, 5) for h in range(CHUNKS)]):
        events.setdefault(min(2 + 4 * i, 31), []).append(functools.partial(p_onward, step, ch))

    g3, f4 = g_ref.reshape(512, 8, 128), f_ref.reshape(384, 2, 8, 128)

    def head(p, carry):
        zero = jnp.zeros((8, 128), jnp.float32)
        one, two = zero, zero
        for m in range(HEAD):
            s, c = sa_s[p, m], sa_c[p, m]
            x = g3[s]
            one = one + x * f4[c, 0]
            two = two + x * f4[c, 1]
        acc_ref[rows_at(p * 16, 8), :] = one
        acc_ref[rows_at(p * 16 + 8, 8), :] = two
        for at, todo in events.items():
            @pl.when(p == at)
            def _():
                for go in todo:
                    go()
        return carry

    lax.fori_loop(0, 32, head, 0)

    p_landed()
    for copy in halo:
        copy.wait_send()
    c_drained()
    p_drained()


def list_kernel(
    g_ref, f_ref, acc_ref, pg_ref, ci_ref, pi_ref, pt_ref,
    child_out, pattern_out, incoming_out,
    ci, pi, child, incoming, sem,
):
    r = lax.axis_index("clus")
    fill_p = pltpu.make_async_copy(pi_ref, pi, sem.at[0])
    fill_c = pltpu.make_async_copy(ci_ref, ci, sem.at[1])
    fill_p.start()
    fill_c.start()
    pattern = pltpu.make_async_copy(pg_ref.at[rows_at(r * 128, 128), :], pattern_out, sem.at[2])
    pattern.start()
    fill_p.wait()

    def parent(p, carry):
        line = lax.rem(r, 2) * 4 + p
        steps = lax.div(pi[PARENT_ROWS + line, 127] + (TAIL - 1), TAIL)

        def step(i, total):
            re, im = total
            for m in range(TAIL):
                s = pl.multiple_of(pi[i * 8 + line, m], 32)
                c = pl.multiple_of(pi[PARENT_ROWS + i * 8 + line, m], 32)
                sr, si = pg_ref[pl.ds(s, 16), :], pg_ref[pl.ds(s + 16, 16), :]
                tr, ti = pt_ref[pl.ds(c, 16), :], pt_ref[pl.ds(c + 16, 16), :]
                re = re + (sr * tr - si * ti)
                im = im + (sr * ti + si * tr)
            return re, im

        zero = jnp.zeros((16, 128), jnp.float32)
        re, im = lax.fori_loop(0, steps, step, (zero, zero))
        incoming[rows_at(p * 32, 16), :] = re
        incoming[rows_at(p * 32 + 16, 16), :] = im
        return carry

    lax.fori_loop(0, 4, parent, 0)
    done = pltpu.make_async_copy(incoming, incoming_out, sem.at[3])
    done.start()
    fill_c.wait()

    def tail(p, carry):
        more = jnp.maximum(ci[CHILD_ROWS + p, 127] - HEAD, 0)
        steps = lax.div(more + (TAIL - 1), TAIL)

        def step(i, total):
            one, two = total
            for m in range(TAIL):
                s = pl.multiple_of(ci[i * 32 + p, m], 8)
                c = pl.multiple_of(ci[CHILD_ROWS + i * 32 + p, m], 16)
                x = g_ref[pl.ds(s, 8), :]
                one = one + x * f_ref[pl.ds(c, 8), :]
                two = two + x * f_ref[pl.ds(c + 8, 8), :]
            return one, two

        start = (acc_ref[rows_at(p * 16, 8), :], acc_ref[rows_at(p * 16 + 8, 8), :])
        one, two = lax.fori_loop(0, steps, step, start)
        child[p, 0] = (one - pltpu.roll(one, 64, 1))[:, :64]
        child[p, 1] = (two + pltpu.roll(two, 64, 1))[:, :64]
        return carry

    lax.fori_loop(0, 32, tail, 0)
    last = pltpu.make_async_copy(child, child_out, sem.at[4])
    last.start()
    pattern.wait()
    done.wait()
    last.wait()


def local(
    child_pattern, child_sources, child_classes, child_counts,
    parent_sources, parent_classes, parent_counts,
    child_table, parent_table, theta_index, theta_weight, phi_index, phi_weight, shift_angle,
):
    f32, i32 = jnp.float32, jnp.int32
    hbm = pl.BlockSpec(memory_space=pltpu.HBM)
    vmem = pl.BlockSpec(memory_space=pltpu.VMEM)
    dma = pltpu.SemaphoreType.DMA
    g, f, acc, pg, ci, pi = pl.pallas_call(
        gather_kernel,
        out_shape=(
            jax.ShapeDtypeStruct((4096, 128), f32),
            jax.ShapeDtypeStruct((6144, 128), f32),
            jax.ShapeDtypeStruct((512, 128), f32),
            jax.ShapeDtypeStruct((2080, 128), f32),
            jax.ShapeDtypeStruct((2 * CHILD_ROWS, 128), i32),
            jax.ShapeDtypeStruct((2 * PARENT_ROWS, 128), i32),
        ),
        in_specs=[hbm] * 13,
        out_specs=(vmem,) * 6,
        scratch_shapes=[
            pltpu.VMEM((32, 2, 8, 64), f32),
            pltpu.VMEM((SLOTS, 128), i32),
            pltpu.VMEM((SLOTS, 128), i32),
            pltpu.VMEM((4, 128), i32),
            pltpu.VMEM((8, SLOTS), i32),
            pltpu.VMEM((8, SLOTS), i32),
            pltpu.SMEM((64,), i32),
            pltpu.VMEM((2, 8, 64, CLASSES), f32),
            pltpu.VMEM((4, 128), i32),
            pltpu.VMEM((4, 128), f32),
            pltpu.VMEM((4, 16), i32),
            pltpu.VMEM((4, 16), f32),
            pltpu.VMEM((128, 128), f32),
            pltpu.VMEM((256, 128), f32),
            pltpu.VMEM((2, 64, 128), f32),
            pltpu.VMEM((2, 64, 128), f32),
            pltpu.VMEM((512, 128), f32),
            pltpu.VMEM((4, 128, 128), i32),
            pltpu.SMEM((32, 128), i32),
            pltpu.SMEM((32, 128), i32),
            dma((13,)),
            dma((2,)),
            dma((2,)),
            dma((2,)),
            dma((2, 4, CHUNKS)),
            dma((8, CHUNKS)),
            dma((8, CHUNKS)),
            dma((8, CHUNKS)),
            dma((2, 4, CHUNKS)),
            dma((8, CHUNKS)),
            dma((8, CHUNKS)),
            dma((8, CHUNKS)),
        ],
        compiler_params=pltpu.CompilerParams(
            collective_id=0, has_side_effects=True, vmem_limit_bytes=24 * 2**20
        ),
        name="gather",
    )(
        child_pattern,
        child_sources.T,
        child_classes.T,
        child_counts.reshape(4, 128),
        parent_sources,
        parent_classes,
        parent_counts,
        child_table.transpose(1, 2, 3, 0),
        theta_index.T,
        theta_weight.T,
        phi_index.T,
        phi_weight.T,
        shift_angle.reshape(128, 128),
    )
    child_incoming, pattern, incoming = pl.pallas_call(
        list_kernel,
        out_shape=(
            jax.ShapeDtypeStruct((32, 2, 8, 64), f32),
            jax.ShapeDtypeStruct((128, 128), f32),
            jax.ShapeDtypeStruct((128, 128), f32),
        ),
        in_specs=[vmem] * 7,
        out_specs=(hbm, hbm, hbm),
        scratch_shapes=[
            pltpu.SMEM((2 * CHILD_ROWS, 128), i32),
            pltpu.SMEM((2 * PARENT_ROWS, 128), i32),
            pltpu.VMEM((32, 2, 8, 64), f32),
            pltpu.VMEM((128, 128), f32),
            dma((5,)),
        ],
        compiler_params=pltpu.CompilerParams(vmem_limit_bytes=24 * 2**20),
        name="lists",
    )(g, f, acc, pg, ci, pi, parent_table.reshape(CLASSES * 32, 128))
    shape = (4, 2, 16, 128)
    return child_incoming, pattern.reshape(shape), incoming.reshape(shape)


def solution(mesh):
    return jax.shard_map(
        local,
        mesh=mesh,
        in_specs=(
            P("clus", None, "ang", None),
            P(), P(), P(), P(), P(), P(),
            P(None, None, "ang", None),
            P(None, None, "ang", None),
            P(), P(),
            P("ang", None),
            P("ang", None),
            P(None, "ang", None),
        ),
        out_specs=(
            P("clus", None, "ang", None),
            P("clus", None, "ang", None),
            P("clus", None, "ang", None),
        ),
        check_vma=False,
    )
```

time: 300 us -> 65.3 us (0.22)
  local copies, waits for them, and re-layouts: 196 us -> 13.4 us
  other arithmetic: 55.1 us -> 0 us
  Pallas kernels: 0 us -> 50.8 us
  waiting for transfers between devices: 25.2 us -> 0 us
  between operations: 14.2 us -> 0.67 us
  starting transfers between devices: 5.92 us -> 0 us
    gather x40 -> x0, local copies, waits for them, and re-layouts: 163 us -> none  [the longest x20 88.5 us: one_block(): factor = table_rows[block_classes]]
    pallas_call x0 -> x2, Pallas kernels: none -> 50.8 us  [the longest x1 42.6 us: local(): pl.pallas_call(gather_kernel, out_shape=(jax.ShapeDtypeStruct((4096, 128)...]
    reduce_sum x15 -> x0, other arithmetic: 43.7 us -> none  [the longest x12 42.2 us: one_block(): real_sum = jnp.sum(jnp.where(live, real_part, 0.0), axis=1)]
    all_gather x2 -> x0, waiting for transfers between devices: 22.1 us -> none  [the longest x1 22.1 us: local(): all_parents = lax.all_gather(parent_flat, 'clus', axis=0, tiled=True)]
    select_n x13 -> x0, other arithmetic: 6.44 us -> none  [the longest x12 5.63 us: one_block(): factor = table_rows[block_classes]]
    ppermute x2 -> x0, starting transfers between devices: 5.84 us -> none  [the longest x1 5.84 us: extended(): lax.ppermute(lax.slice_in_dim(block, 0, width, axis=dim), axis, backward)]
    lt x8 -> x0, local copies, waits for them, and re-layouts: 5.52 us -> none  [one_block(): jnp.arange(slot_count, dtype=jnp.int32)[None, :] < block_counts[:, None]]
    dynamic_slice x9 -> x0, local copies, waits for them, and re-layouts: 4.98 us -> none  [the longest x4 2.32 us: apply_lists(): lax.map(one_block, (source_ids.reshape(blocks, -1, slot_count), class_ids...]
  transfers between devices with their start and end apart: 4 -> 0, of which waited for: 2 -> 0; matrix products, arithmetic and copies ran while one was open for 28% -> 0% of each run, Pallas kernels for 0% -> 0%
where the time goes in v1:
time: 65.3 us; the launch traced here: 64.8 us
  Pallas kernels  50.8 us (78%)
  local copies, waits for them, and re-layouts  13.4 us (21%)
  between operations  0.67 us (1%)
    pallas_call x1, Pallas kernels, local(): pl.pallas_call(gather_kernel, out_shape=(jax.ShapeDtypeStruct((4096, 128)...  42.6 us
    unnamed x28, local copies, waits for them, and re-layouts  13.4 us
    pallas_call x1, Pallas kernels, local(): pl.pallas_call(list_kernel, out_shape=(jax.ShapeDtypeStruct((32, 2, 8, 64...  8.13 us

profile of v1, /device:TPU:1, one launch (start us, length us, event | category | flops | bytes accessed | tf_op | source)
XLA Modules:
  0.0 64.8 jit_solution(10078018709115906597)
XLA Ops:
  0.6 0.0 copy-start.1
  0.6 1.4 %copy-done.1 = f32[316,2,8,64]{0,3,2,1:T(8,128)S(1)} copy-done((f32[316,2,8,64]{0,3,2,1:T(8,128)S(1)}, f32[316,2,8,64]{0,3,2,1:T(8,128)}, u32[]{:S(2)}) %copy-start.1) | copy-done | bytes 1294360
  2.0 0.0 copy-start.2
  2.0 1.0 %copy-done.2 = s32[512,189]{0,1:T(8,128)S(1)} copy-done((s32[512,189]{0,1:T(8,128)S(1)}, s32[512,189]{0,1:T(8,128)}, u32[]{:S(2)}) %copy-start.2) | copy-done | bytes 387096
  3.0 0.0 copy-start.3
  3.0 1.0 %copy-done.3 = s32[512,189]{0,1:T(8,128)S(1)} copy-done((s32[512,189]{0,1:T(8,128)S(1)}, s32[512,189]{0,1:T(8,128)}, u32[]{:S(2)}) %copy-start.3) | copy-done | bytes 387096
  4.0 0.0 copy-start.4
  4.0 0.9 %copy-done.4 = f32[32,2,8,64]{3,2,1,0:T(8,128)S(1)} copy-done((f32[32,2,8,64]{3,2,1,0:T(8,128)S(1)}, f32[32,2,8,64]{3,2,1,0:T(8,128)}, u32[]{:S(2)}) %copy-start.4) | copy-done | bytes 131096
  5.0 0.0 copy-start.5
  5.0 0.8 %copy-done.5 = s32[64,189]{1,0:T(8,128)S(1)} copy-done((s32[64,189]{1,0:T(8,128)S(1)}, s32[64,189]{1,0:T(8,128)}, u32[]{:S(2)}) %copy-start.5) | copy-done | bytes 48408
  5.8 0.0 copy-start.6
  5.8 0.8 %copy-done.6 = s32[64,189]{1,0:T(8,128)S(1)} copy-done((s32[64,189]{1,0:T(8,128)S(1)}, s32[64,189]{1,0:T(8,128)}, u32[]{:S(2)}) %copy-start.6) | copy-done | bytes 48408
  6.7 0.0 copy-start.7
  6.7 0.8 %copy-done.7 = f32[8,16,128]{2,1,0:T(8,128)S(1)} copy-done((f32[8,16,128]{2,1,0:T(8,128)S(1)}, f32[8,16,128]{2,1,0:T(8,128)}, u32[]{:S(2)}) %copy-start.7) | copy-done | bytes 65560
  7.5 0.0 copy-start.8
  7.5 0.7 %copy-done.8 = s32[512]{0:T(512)S(1)} copy-done((s32[512]{0:T(512)S(1)}, s32[512]{0:T(512)}, u32[]{:S(2)}) %copy-start.8) | copy-done | bytes 2072
  8.2 0.0 copy-start.9
  8.2 0.7 %copy-done.9 = s32[128,4]{0,1:T(4,128)S(1)} copy-done((s32[128,4]{0,1:T(4,128)S(1)}, s32[128,4]{0,1:T(4,128)}, u32[]{:S(2)}) %copy-start.9) | copy-done | bytes 2072
  8.9 0.0 copy-start.10
  8.9 0.7 %copy-done.10 = f32[128,4]{0,1:T(4,128)S(1)} copy-done((f32[128,4]{0,1:T(4,128)S(1)}, f32[128,4]{0,1:T(4,128)}, u32[]{:S(2)}) %copy-start.10) | copy-done | bytes 2072
  9.6 0.0 copy-start.11
  9.6 0.7 %copy-done.11 = s32[16,4]{0,1:T(4,128)S(1)} copy-done((s32[16,4]{0,1:T(4,128)S(1)}, s32[16,4]{0,1:T(4,128)}, u32[]{:S(2)}) %copy-start.11) | copy-done | bytes 280
  10.2 0.0 copy-start.12
  10.2 0.7 %copy-done.12 = f32[16,4]{0,1:T(4,128)S(1)} copy-done((f32[16,4]{0,1:T(4,128)S(1)}, f32[16,4]{0,1:T(4,128)}, u32[]{:S(2)}) %copy-start.12) | copy-done | bytes 280
  10.9 0.0 copy-start.13
  10.9 0.7 %copy-done.13 = s32[64]{0:T(128)S(1)} copy-done((s32[64]{0:T(128)S(1)}, s32[64]{0:T(128)}, u32[]{:S(2)}) %copy-start.13) | copy-done | bytes 280
  11.6 42.6 %gather.1 = (f32[4096,128]{1,0:T(8,128)S(1)}, f32[6144,128]{1,0:T(8,128)S(1)}, f32[512,128]{1,0:T(8,128)S(1)}, f32[2080,128]{1,0:T(8,128)S(1)}, s32[192,128]{1,0:T(8,128)S(1)}, /*index=5*/s32[96,128]{1,0:T(8,128)S(1)}) custom-call(f32[32,2,8,64]{3,2,1,0:T(8,128)S(1)} %copy-done.4, s32[189,512]{1,0:T(8,128)S(1)} %bitcast.14, s32[189,512]{1,0:T(8,128)S(1)} %bitcast.15, ...), custom_call_target="tpu_custom_call" | custom-call | tf_op jit(solution)/shard_map/gather/pallas_call | solution.py:407
  54.2 0.0 copy-start
  54.2 2.5 %copy-done = f32[316,2,16,128]{3,2,1,0:T(8,128)S(1)} copy-done((f32[316,2,16,128]{3,2,1,0:T(8,128)S(1)}, f32[316,2,16,128]{3,2,1,0:T(8,128)}, u32[]{:S(2)}) %copy-start) | copy-done | bytes 5177368
  56.7 8.1 %lists.1 = (f32[32,2,8,64]{3,2,1,0:T(8,128)}, f32[128,128]{1,0:T(8,128)}, f32[128,128]{1,0:T(8,128)}) custom-call(f32[4096,128]{1,0:T(8,128)S(1)} %get-tuple-element.12.g_ref, f32[6144,128]{1,0:T(8,128)S(1)} %get-tuple-element.13.f_ref, f32[512,128]{1,0:T(8,128)S(1)} %get-tuple-element.14.acc_ref, f32[2080,128]{1,0:T(8,128)S(1)} %get-tuple-element.15.pg_ref, ...), custom_call_target="tpu_custom_call" | custom-call | tf_op jit(solution)/shard_map/lists/pallas_call | solution.py:472
Async XLA Ops:
  0.6 1.4 %copy-start.1 = (f32[316,2,8,64]{0,3,2,1:T(8,128)S(1)}, f32[316,2,8,64]{0,3,2,1:T(8,128)}, u32[]{:S(2)}) copy-start(f32[316,2,8,64]{0,3,2,1:T(8,128)} %param.21) | copy-start | bytes 3883012
  2.0 1.0 %copy-start.2 = (s32[512,189]{0,1:T(8,128)S(1)}, s32[512,189]{0,1:T(8,128)}, u32[]{:S(2)}) copy-start(s32[512,189]{0,1:T(8,128)} %param.15) | copy-start | bytes 1161220
  3.0 1.0 %copy-start.3 = (s32[512,189]{0,1:T(8,128)S(1)}, s32[512,189]{0,1:T(8,128)}, u32[]{:S(2)}) copy-start(s32[512,189]{0,1:T(8,128)} %param.16) | copy-start | bytes 1161220
  4.0 0.9 %copy-start.4 = (f32[32,2,8,64]{3,2,1,0:T(8,128)S(1)}, f32[32,2,8,64]{3,2,1,0:T(8,128)}, u32[]{:S(2)}) copy-start(f32[32,2,8,64]{3,2,1,0:T(8,128)} %pat_hbm.1) | copy-start | bytes 393220
  5.0 0.8 %copy-start.5 = (s32[64,189]{1,0:T(8,128)S(1)}, s32[64,189]{1,0:T(8,128)}, u32[]{:S(2)}) copy-start(s32[64,189]{1,0:T(8,128)} %ps_hbm.1) | copy-start | bytes 145156
  5.8 0.8 %copy-start.6 = (s32[64,189]{1,0:T(8,128)S(1)}, s32[64,189]{1,0:T(8,128)}, u32[]{:S(2)}) copy-start(s32[64,189]{1,0:T(8,128)} %pc_hbm.1) | copy-start | bytes 145156
  6.7 0.8 %copy-start.7 = (f32[8,16,128]{2,1,0:T(8,128)S(1)}, f32[8,16,128]{2,1,0:T(8,128)}, u32[]{:S(2)}) copy-start(f32[8,16,128]{2,1,0:T(8,128)} %param.27) | copy-start | bytes 196612
  7.5 0.7 %copy-start.8 = (s32[512]{0:T(512)S(1)}, s32[512]{0:T(512)}, u32[]{:S(2)}) copy-start(s32[512]{0:T(512)} %param.17) | copy-start | bytes 6148
  8.2 0.7 %copy-start.9 = (s32[128,4]{0,1:T(4,128)S(1)}, s32[128,4]{0,1:T(4,128)}, u32[]{:S(2)}) copy-start(s32[128,4]{0,1:T(4,128)} %param.23) | copy-start | bytes 6148
  8.9 0.7 %copy-start.10 = (f32[128,4]{0,1:T(4,128)S(1)}, f32[128,4]{0,1:T(4,128)}, u32[]{:S(2)}) copy-start(f32[128,4]{0,1:T(4,128)} %param.24) | copy-start | bytes 6148
  9.6 0.7 %copy-start.11 = (s32[16,4]{0,1:T(4,128)S(1)}, s32[16,4]{0,1:T(4,128)}, u32[]{:S(2)}) copy-start(s32[16,4]{0,1:T(4,128)} %param.25) | copy-start | bytes 772
  10.2 0.7 %copy-start.12 = (f32[16,4]{0,1:T(4,128)S(1)}, f32[16,4]{0,1:T(4,128)}, u32[]{:S(2)}) copy-start(f32[16,4]{0,1:T(4,128)} %param.26) | copy-start | bytes 772
  10.9 0.7 %copy-start.13 = (s32[64]{0:T(128)S(1)}, s32[64]{0:T(128)}, u32[]{:S(2)}) copy-start(s32[64]{0:T(128)} %pcnt_hbm.1) | copy-start | bytes 772
  54.2 2.5 %copy-start = (f32[316,2,16,128]{3,2,1,0:T(8,128)S(1)}, f32[316,2,16,128]{3,2,1,0:T(8,128)}, u32[]{:S(2)}) copy-start(f32[316,2,16,128]{3,2,1,0:T(8,128)} %param.22) | copy-start | bytes 15532036

commit v2 on v1

--- a/solution.py
+++ b/solution.py
@@ -453,8 +453,9 @@
         compiler_params=pltpu.CompilerParams(
             collective_id=0, has_side_effects=True, vmem_limit_bytes=24 * 2**20
         ),
+        cost_estimate=pl.CostEstimate(flops=30_000_000_000, bytes_accessed=8_000_000, transcendentals=0),
         name="gather",
-    )(
+    )(*(pltpu.with_memory_space_constraint(x, pltpu.HBM) for x in (
         child_pattern,
         child_sources.T,
         child_classes.T,
@@ -468,7 +469,7 @@
         phi_index.T,
         phi_weight.T,
         shift_angle.reshape(128, 128),
-    )
+    )))
     child_incoming, pattern, incoming = pl.pallas_call(
         list_kernel,
         out_shape=(

time: 65.3 us -> 50.1 us (0.77)
  local copies, waits for them, and re-layouts: 13.4 us -> 0.01 us
  Pallas kernels: 50.8 us -> 49.3 us
    unnamed x28 -> x4, local copies, waits for them, and re-layouts: 13.4 us -> 0.01 us
    pallas_call x1, Pallas kernels: 8.13 us -> 6.71 us  [local(): pl.pallas_call(list_kernel, out_shape=(jax.ShapeDtypeStruct((32, 2, 8, 64...]
where the time goes in v2:
time: 50.1 us; the launch traced here: 50 us
  Pallas kernels  49.3 us (98%)
  between operations  0.68 us (1%)
    pallas_call x1, Pallas kernels, local(): pl.pallas_call(gather_kernel, out_shape=(jax.ShapeDtypeStruct((4096, 128)...  42.6 us
    pallas_call x1, Pallas kernels, local(): pl.pallas_call(list_kernel, out_shape=(jax.ShapeDtypeStruct((32, 2, 8, 64...  6.71 us

profile of v2, /device:TPU:1, one launch (start us, length us, event | category | flops | bytes accessed | tf_op | source)
XLA Modules:
  0.0 50.0 jit_solution(3438972907922635704)
XLA Ops:
  0.6 0.0 slice-start
  0.6 0.0 slice-start.1
  0.7 42.6 %gather.1 = (f32[4096,128]{1,0:T(8,128)S(1)}, f32[6144,128]{1,0:T(8,128)S(1)}, f32[512,128]{1,0:T(8,128)S(1)}, f32[2080,128]{1,0:T(8,128)S(1)}, s32[192,128]{1,0:T(8,128)S(1)}, /*index=5*/s32[96,128]{1,0:T(8,128)S(1)}) custom-call(f32[32,2,8,64]{3,2,1,0:T(8,128)} %pat_hbm.1, s32[189,512]{1,0:T(8,128)} %bitcast.16, s32[189,512]{1,0:T(8,128)} %bitcast.17, ...), custom_call_target="tpu_custom_call" | custom-call | flops 30000001024 | bytes 8000000 | tf_op jit(solution)/shard_map/gather/pallas_call | solution.py:407
  43.3 0.0 slice-done
  43.3 0.0 slice-done.1
  43.3 6.7 %lists.1 = (f32[32,2,8,64]{3,2,1,0:T(8,128)}, f32[128,128]{1,0:T(8,128)}, f32[128,128]{1,0:T(8,128)}) custom-call(f32[4096,128]{1,0:T(8,128)S(1)} %get-tuple-element.12.g_ref, f32[6144,128]{1,0:T(8,128)S(1)} %get-tuple-element.13.f_ref, f32[512,128]{1,0:T(8,128)S(1)} %get-tuple-element.14.acc_ref, f32[2080,128]{1,0:T(8,128)S(1)} %get-tuple-element.15.pg_ref, ...), custom_call_target="tpu_custom_call" | custom-call | tf_op jit(solution)/shard_map/lists/pallas_call | solution.py:473
  (1 shorter events, 0.0 us)
Async XLA Ops:
  0.6 42.6 %slice-start = ((s8[5177344]{0:T(1024)(128)(4,1)}), s8[4194304]{0:T(1024)(128)(4,1)S(1)}, s32[]{:S(2)}) async-start(s8[5177344]{0:T(1024)(128)(4,1)} %bitcast.12), calls=%async_computation | async-start | bytes 8388608
  0.6 42.6 %slice-start.1 = ((s8[5177344]{0:T(1024)(128)(4,1)}), s8[983040]{0:T(1024)(128)(4,1)S(1)}, s32[]{:S(2)}) async-start(s8[5177344]{0:T(1024)(128)(4,1)} %bitcast.12), calls=%async_computation.1 | async-start | bytes 1966080

commit v3 on v2

--- a/solution.py
+++ b/solution.py
@@ -10,13 +10,10 @@
 MESH = pl.DeviceIdType.MESH
 SLOTS = 189
 CLASSES = 316
-HEAD = 96
-TAIL = 32
+HEAD = 64
+CHILD_TAIL = 25
+PARENT_TAIL = 27
 CHUNKS = 2
-CHILD_STEPS = -(-(SLOTS - HEAD) // TAIL)
-PARENT_STEPS = -(-SLOTS // TAIL)
-CHILD_ROWS = 32 * CHILD_STEPS
-PARENT_ROWS = 8 * PARENT_STEPS
 
 
 def rows_at(start, size):
@@ -28,7 +25,7 @@
     thi_hbm, thw_hbm, phi_hbm, phw_hbm, ang_hbm,
     g_ref, f_ref, acc_ref, pg_ref, ci_ref, pi_ref,
     pat, sv, cv, ccnt, psv, pcv, pcnt, tab, thi, thw, phi, phw, ang,
-    own, hs, hr, zs, ta, sa_s, sa_c,
+    own, hs, hr, zs, pair, turns, ta, sa_s, sa_c,
     loc, smsem, hsend, hrecv, csend, crecv, cssend, csrecv, psend, precv, pssend, psrecv,
 ):
     r = lax.axis_index("clus")
@@ -153,6 +150,58 @@
         copy.start()
         halo.append(copy)
 
+    for i in (7, 8, 9, 10, 11):
+        copies[i].wait()
+    row = lax.broadcasted_iota(jnp.int32, (64, 128), 0)
+    theta = jnp.zeros((64, 128), jnp.float32)
+    for i in range(4):
+        theta = theta + jnp.where(thi[i:i + 1, :] == row, thw[i:i + 1, :], 0.0)
+    blank = jnp.zeros((64, 128), jnp.float32)
+    pair[...] = jnp.concatenate(
+        [jnp.concatenate([theta, blank], axis=1), jnp.concatenate([blank, theta], axis=1)], axis=0
+    )
+    angles = ang[...]
+    turns[0] = jnp.cos(angles)
+    turns[1] = jnp.sin(angles)
+    offset = lax.rem(phi[...] - a * 8 + (2 + 128), 128)
+    weights = phw[...]
+    base = lax.shift_right_logical(lax.broadcasted_iota(jnp.int32, (1, 16), 1), 1)
+    taps = []
+    for d in range(5):
+        tap = jnp.zeros((1, 16), jnp.float32)
+        for i in range(4):
+            tap = tap + jnp.where(offset[i:i + 1, :] == base + d, weights[i:i + 1, :], 0.0)
+        taps.append(tap)
+
+    for copy in halo:
+        copy.wait_recv()
+    cols = [hr[0, :32, :], hr[0, 32:, :]]
+    cols += [own[pl.ds(j, 32, stride=8), :] for j in range(8)]
+    cols += [hr[1, :32, :], hr[1, 32:, :]]
+    for j in range(16):
+        z = jnp.zeros((32, 128), jnp.float32)
+        for d in range(5):
+            z = z + taps[d][:, j:j + 1] * cols[j // 2 + d]
+        zs[pl.ds(j, 32, stride=16), :] = z
+
+    for parent in range(4):
+        y = jnp.dot(
+            zs[parent * 128:(parent + 1) * 128, :], pair[...],
+            precision=lax.Precision.HIGHEST, preferred_element_type=jnp.float32,
+        )
+        re = y[:, :128] * turns[0] - y[:, 128:] * turns[1]
+        im = y[:, :128] * turns[1] + y[:, 128:] * turns[0]
+        re = jnp.sum(re.reshape(8, 16, 128), axis=0)
+        im = jnp.sum(im.reshape(8, 16, 128), axis=0)
+        pg_ref[rows_at(r * 128 + parent * 32, 16), :] = re
+        pg_ref[rows_at(r * 128 + parent * 32 + 16, 16), :] = im
+        if parent == 1:
+            c_onward(1, 0)
+            c_onward(1, 1)
+            p_first(0)
+    p_first(1)
+    pg_ref[2048:2080, :] = jnp.zeros((32, 128), jnp.float32)
+
     for i in (1, 2, 3):
         copies[i].wait()
     count_row = ccnt[pl.ds(lax.div(r, 4), 1), :]
@@ -162,13 +211,11 @@
     def lists(start, stop):
         s, c = sv[start:stop, :], cv[start:stop, :]
         live = slot[:stop - start] + start < count_row
-        s = jnp.where(live, s, 0) * 8
-        c = jnp.where(live, c, CLASSES) * 16
-        return s, c
+        return jnp.where(live, s, 0), jnp.where(live, c, CLASSES)
 
     s, c = lists(0, 128)
-    ta[0] = lax.shift_right_logical(s, 3).T
-    ta[1] = lax.shift_right_logical(c, 4).T
+    ta[0] = s.T
+    ta[1] = c.T
     fill = [
         pltpu.make_async_copy(ta.at[0, own_rows, :], sa_s, smsem.at[0]),
         pltpu.make_async_copy(ta.at[1, own_rows, :], sa_c, smsem.at[1]),
@@ -176,21 +223,18 @@
     for copy in fill:
         copy.start()
 
-    c_onward(1, 0)
-
     s, c = lists(HEAD, SLOTS)
     rest = 128 - (SLOTS - HEAD)
-    s = jnp.concatenate([s, jnp.zeros((rest, 128), jnp.int32)], axis=0)
-    c = jnp.concatenate([c, jnp.full((rest, 128), CLASSES * 16, jnp.int32)], axis=0)
+    s = jnp.concatenate([s * 8, jnp.zeros((rest, 128), jnp.int32)], axis=0)
+    c = jnp.concatenate([c * 16, jnp.full((rest, 128), CLASSES * 16, jnp.int32)], axis=0)
     c = jnp.where(slot == 127, count_row, c)
     ta[2] = s.T
     ta[3] = c.T
-    ts, tc = ta[2, own_rows, :], ta[3, own_rows, :]
-    for i in range(CHILD_STEPS):
-        ci_ref[i * 32:(i + 1) * 32, :] = pltpu.roll(ts, (128 - i * TAIL) % 128, 1) if i else ts
-        ci_ref[CHILD_ROWS + i * 32:CHILD_ROWS + (i + 1) * 32, :] = (
-            pltpu.roll(tc, (128 - i * TAIL) % 128, 1) if i else tc
-        )
+    ci_ref[:32, :] = ta[2, own_rows, :]
+    ci_ref[32:, :] = ta[3, own_rows, :]
+
+    c_onward(2, 0)
+    c_onward(2, 1)
 
     for i in (4, 5, 6):
         copies[i].wait()
@@ -209,15 +253,11 @@
         live = lane + half * 128 < counts
         s = jnp.where(live, s, 64) * 32
         c = jnp.where(live, c, 0) * 32
-        for i in range(half * 128 // TAIL, min((half + 1) * 128 // TAIL, PARENT_STEPS)):
-            turn = (128 - (i * TAIL - half * 128)) % 128
-            si = pltpu.roll(s, turn, 1) if turn else s
-            cj = pltpu.roll(c, turn, 1) if turn else c
-            pi_ref[i * 8:(i + 1) * 8, :] = si
-            pi_ref[PARENT_ROWS + i * 8:PARENT_ROWS + (i + 1) * 8, :] = jnp.where(lane == 127, counts, cj)
-    pg_ref[2048:2080, :] = jnp.zeros((32, 128), jnp.float32)
-
-    c_onward(1, 1)
+        pi_ref[half * 8:half * 8 + 8, :] = s
+        pi_ref[16 + half * 8:16 + half * 8 + 8, :] = jnp.where(lane == 127, counts, c) if half else c
+
+    p_onward(1, 0)
+    p_onward(1, 1)
 
     copies[12].wait()
 
@@ -233,71 +273,22 @@
 
     for col in range(4):
         operators(col)
-    c_onward(2, 0)
+    c_onward(3, 0)
+    c_onward(3, 1)
     for col in range(4, 8):
         operators(col)
-    c_onward(2, 1)
-
-    for i in (7, 8, 9, 10, 11):
-        copies[i].wait()
-    for copy in halo:
-        copy.wait_recv()
-    offset = lax.rem(phi[...] - a * 8 + (2 + 128), 128)
-    weights = phw[...]
-    base = lax.shift_right_logical(lax.broadcasted_iota(jnp.int32, (1, 16), 1), 1)
-    taps = []
-    for d in range(5):
-        tap = jnp.zeros((1, 16), jnp.float32)
-        for i in range(4):
-            tap = tap + jnp.where(offset[i:i + 1, :] == base + d, weights[i:i + 1, :], 0.0)
-        taps.append(tap)
-    cols = [hr[0, :32, :], hr[0, 32:, :]]
-    cols += [own[pl.ds(j, 32, stride=8), :] for j in range(8)]
-    cols += [hr[1, :32, :], hr[1, 32:, :]]
-    for j in range(16):
-        z = jnp.zeros((32, 128), jnp.float32)
-        for d in range(5):
-            z = z + taps[d][:, j:j + 1] * cols[j // 2 + d]
-        zs[pl.ds(j, 32, stride=16), :] = z
-
-    c_onward(3, 0)
-
-    row = lax.broadcasted_iota(jnp.int32, (64, 128), 0)
-    theta = jnp.zeros((64, 128), jnp.float32)
-    for i in range(4):
-        theta = theta + jnp.where(thi[i:i + 1, :] == row, thw[i:i + 1, :], 0.0)
-    blank = jnp.zeros((64, 128), jnp.float32)
-    pair = jnp.concatenate(
-        [jnp.concatenate([theta, blank], axis=1), jnp.concatenate([blank, theta], axis=1)], axis=0
-    )
-    angles = ang[...]
-    cosine, sine = jnp.cos(angles), jnp.sin(angles)
-
-    c_onward(3, 1)
-
-    for parent in range(4):
-        y = jnp.dot(
-            zs[parent * 128:(parent + 1) * 128, :], pair,
-            precision=lax.Precision.HIGHEST, preferred_element_type=jnp.float32,
-        )
-        re = y[:, :128] * cosine - y[:, 128:] * sine
-        im = y[:, :128] * sine + y[:, 128:] * cosine
-        re = jnp.sum(re.reshape(8, 16, 128), axis=0)
-        im = jnp.sum(im.reshape(8, 16, 128), axis=0)
-        pg_ref[rows_at(r * 128 + parent * 32, 16), :] = re
-        pg_ref[rows_at(r * 128 + parent * 32 + 16, 16), :] = im
-        if parent % 2:
-            p_first(parent // 2)
+    p_onward(2, 0)
+    p_onward(2, 1)
 
     for ch in range(CHUNKS):
         c_onward(4, ch)
     for copy in fill:
         copy.wait()
     c_landed()
-
-    events = {}
-    for i, (step, ch) in enumerate([(s, h) for s in range(1, 5) for h in range(CHUNKS)]):
-        events.setdefault(min(2 + 4 * i, 31), []).append(functools.partial(p_onward, step, ch))
+    p_onward(3, 0)
+    p_onward(3, 1)
+
+    events = {16: [functools.partial(p_onward, 4, ch) for ch in range(CHUNKS)]}
 
     g3, f4 = g_ref.reshape(512, 8, 128), f_ref.reshape(384, 2, 8, 128)
 
@@ -341,15 +332,25 @@
     pattern.start()
     fill_p.wait()
 
+    def run(count, width, last, chunk, total, start=0):
+        if start >= last:
+            return total
+        stop = min(start + width, last)
+
+        def more(total):
+            return run(count, width, last, chunk, chunk(start, stop, total), stop)
+
+        return lax.cond(count > start, more, lambda total: total, total)
+
     def parent(p, carry):
         line = lax.rem(r, 2) * 4 + p
-        steps = lax.div(pi[PARENT_ROWS + line, 127] + (TAIL - 1), TAIL)
-
-        def step(i, total):
+
+        def chunk(start, stop, total):
             re, im = total
-            for m in range(TAIL):
-                s = pl.multiple_of(pi[i * 8 + line, m], 32)
-                c = pl.multiple_of(pi[PARENT_ROWS + i * 8 + line, m], 32)
+            for m in range(start, stop):
+                row = line + 8 * (m // 128)
+                s = pl.multiple_of(pi[row, m % 128], 32)
+                c = pl.multiple_of(pi[16 + row, m % 128], 32)
                 sr, si = pg_ref[pl.ds(s, 16), :], pg_ref[pl.ds(s + 16, 16), :]
                 tr, ti = pt_ref[pl.ds(c, 16), :], pt_ref[pl.ds(c + 16, 16), :]
                 re = re + (sr * tr - si * ti)
@@ -357,7 +358,7 @@
             return re, im
 
         zero = jnp.zeros((16, 128), jnp.float32)
-        re, im = lax.fori_loop(0, steps, step, (zero, zero))
+        re, im = run(pi[24 + line, 127], PARENT_TAIL, SLOTS, chunk, (zero, zero))
         incoming[rows_at(p * 32, 16), :] = re
         incoming[rows_at(p * 32 + 16, 16), :] = im
         return carry
@@ -368,21 +369,18 @@
     fill_c.wait()
 
     def tail(p, carry):
-        more = jnp.maximum(ci[CHILD_ROWS + p, 127] - HEAD, 0)
-        steps = lax.div(more + (TAIL - 1), TAIL)
-
-        def step(i, total):
+        def chunk(start, stop, total):
             one, two = total
-            for m in range(TAIL):
-                s = pl.multiple_of(ci[i * 32 + p, m], 8)
-                c = pl.multiple_of(ci[CHILD_ROWS + i * 32 + p, m], 16)
+            for m in range(start, stop):
+                s = pl.multiple_of(ci[p, m], 8)
+                c = pl.multiple_of(ci[32 + p, m], 16)
                 x = g_ref[pl.ds(s, 8), :]
                 one = one + x * f_ref[pl.ds(c, 8), :]
                 two = two + x * f_ref[pl.ds(c + 8, 8), :]
             return one, two
 
         start = (acc_ref[rows_at(p * 16, 8), :], acc_ref[rows_at(p * 16 + 8, 8), :])
-        one, two = lax.fori_loop(0, steps, step, start)
+        one, two = run(ci[32 + p, 127] - HEAD, CHILD_TAIL, SLOTS - HEAD, chunk, start)
         child[p, 0] = (one - pltpu.roll(one, 64, 1))[:, :64]
         child[p, 1] = (two + pltpu.roll(two, 64, 1))[:, :64]
         return carry
@@ -411,8 +409,8 @@
             jax.ShapeDtypeStruct((6144, 128), f32),
             jax.ShapeDtypeStruct((512, 128), f32),
             jax.ShapeDtypeStruct((2080, 128), f32),
-            jax.ShapeDtypeStruct((2 * CHILD_ROWS, 128), i32),
-            jax.ShapeDtypeStruct((2 * PARENT_ROWS, 128), i32),
+            jax.ShapeDtypeStruct((64, 128), i32),
+            jax.ShapeDtypeStruct((32, 128), i32),
         ),
         in_specs=[hbm] * 13,
         out_specs=(vmem,) * 6,
@@ -434,6 +432,8 @@
             pltpu.VMEM((2, 64, 128), f32),
             pltpu.VMEM((2, 64, 128), f32),
             pltpu.VMEM((512, 128), f32),
+            pltpu.VMEM((128, 256), f32),
+            pltpu.VMEM((2, 128, 128), f32),
             pltpu.VMEM((4, 128, 128), i32),
             pltpu.SMEM((32, 128), i32),
             pltpu.SMEM((32, 128), i32),
@@ -480,8 +480,8 @@
         in_specs=[vmem] * 7,
         out_specs=(hbm, hbm, hbm),
         scratch_shapes=[
-            pltpu.SMEM((2 * CHILD_ROWS, 128), i32),
-            pltpu.SMEM((2 * PARENT_ROWS, 128), i32),
+            pltpu.SMEM((64, 128), i32),
+            pltpu.SMEM((32, 128), i32),
             pltpu.VMEM((32, 2, 8, 64), f32),
             pltpu.VMEM((128, 128), f32),
             dma((5,)),

time: 50.1 us -> 41.6 us (0.83)
  Pallas kernels: 49.3 us -> 40.8 us
    pallas_call x1, Pallas kernels: 42.6 us -> 35.8 us  [local(): pl.pallas_call(gather_kernel, out_shape=(jax.ShapeDtypeStruct((4096, 128)...]
    pallas_call x1, Pallas kernels: 6.71 us -> 5.02 us  [local(): pl.pallas_call(list_kernel, out_shape=(jax.ShapeDtypeStruct((32, 2, 8, 64...]
where the time goes in v3:
time: 41.6 us; the launch traced here: 41.5 us
  Pallas kernels  40.8 us (98%)
  between operations  0.68 us (2%)
    pallas_call x1, Pallas kernels, local(): pl.pallas_call(gather_kernel, out_shape=(jax.ShapeDtypeStruct((4096, 128)...  35.8 us
    pallas_call x1, Pallas kernels, local(): pl.pallas_call(list_kernel, out_shape=(jax.ShapeDtypeStruct((32, 2, 8, 64...  5.02 us

profile of v3, /device:TPU:1, one launch (start us, length us, event | category | flops | bytes accessed | tf_op | source)
XLA Modules:
  0.0 41.5 jit_solution(10153329212296343474)
XLA Ops:
  0.6 0.0 slice-start
  0.6 0.0 slice-start.1
  0.7 35.8 %gather.1 = (f32[4096,128]{1,0:T(8,128)S(1)}, f32[6144,128]{1,0:T(8,128)S(1)}, f32[512,128]{1,0:T(8,128)S(1)}, f32[2080,128]{1,0:T(8,128)S(1)}, s32[64,128]{1,0:T(8,128)S(1)}, /*index=5*/s32[32,128]{1,0:T(8,128)S(1)}) custom-call(f32[32,2,8,64]{3,2,1,0:T(8,128)} %pat_hbm.1, s32[189,512]{1,0:T(8,128)} %bitcast.16, s32[189,512]{1,0:T(8,128)} %bitcast.17, ...), custom_call_target="tpu_custom_call" | custom-call | flops 30000001024 | bytes 8000000 | tf_op jit(solution)/shard_map/gather/pallas_call | solution.py:405
  36.5 0.0 slice-done
  36.5 0.0 slice-done.1
  36.5 5.0 %lists.1 = (f32[32,2,8,64]{3,2,1,0:T(8,128)}, f32[128,128]{1,0:T(8,128)}, f32[128,128]{1,0:T(8,128)}) custom-call(f32[4096,128]{1,0:T(8,128)S(1)} %get-tuple-element.12.g_ref, f32[6144,128]{1,0:T(8,128)S(1)} %get-tuple-element.13.f_ref, f32[512,128]{1,0:T(8,128)S(1)} %get-tuple-element.14.acc_ref, f32[2080,128]{1,0:T(8,128)S(1)} %get-tuple-element.15.pg_ref, ...), custom_call_target="tpu_custom_call" | custom-call | tf_op jit(solution)/shard_map/lists/pallas_call | solution.py:473
  (1 shorter events, 0.0 us)
Async XLA Ops:
  0.6 35.8 %slice-start = ((s8[5177344]{0:T(1024)(128)(4,1)}), s8[4194304]{0:T(1024)(128)(4,1)S(1)}, s32[]{:S(2)}) async-start(s8[5177344]{0:T(1024)(128)(4,1)} %bitcast.12), calls=%async_computation | async-start | bytes 8388608
  0.6 35.8 %slice-start.1 = ((s8[5177344]{0:T(1024)(128)(4,1)}), s8[983040]{0:T(1024)(128)(4,1)S(1)}, s32[]{:S(2)}) async-start(s8[5177344]{0:T(1024)(128)(4,1)} %bitcast.12), calls=%async_computation.1 | async-start | bytes 1966080

commit v4 on v3

--- a/solution.py
+++ b/solution.py
@@ -25,7 +25,7 @@
     thi_hbm, thw_hbm, phi_hbm, phw_hbm, ang_hbm,
     g_ref, f_ref, acc_ref, pg_ref, ci_ref, pi_ref,
     pat, sv, cv, ccnt, psv, pcv, pcnt, tab, thi, thw, phi, phw, ang,
-    own, hs, hr, zs, pair, turns, ta, sa_s, sa_c,
+    own, hs, hr, zs, pair, turns, pv, ta, sa_s, sa_c,
     loc, smsem, hsend, hrecv, csend, crecv, cssend, csrecv, psend, precv, pssend, psrecv,
 ):
     r = lax.axis_index("clus")
@@ -230,8 +230,12 @@
     c = jnp.where(slot == 127, count_row, c)
     ta[2] = s.T
     ta[3] = c.T
-    ci_ref[:32, :] = ta[2, own_rows, :]
-    ci_ref[32:, :] = ta[3, own_rows, :]
+    fill += [
+        pltpu.make_async_copy(ta.at[2, own_rows, :], ci_ref.at[:32, :], smsem.at[2]),
+        pltpu.make_async_copy(ta.at[3, own_rows, :], ci_ref.at[32:, :], smsem.at[3]),
+    ]
+    fill[2].start()
+    fill[3].start()
 
     c_onward(2, 0)
     c_onward(2, 1)
@@ -253,8 +257,11 @@
         live = lane + half * 128 < counts
         s = jnp.where(live, s, 64) * 32
         c = jnp.where(live, c, 0) * 32
-        pi_ref[half * 8:half * 8 + 8, :] = s
-        pi_ref[16 + half * 8:16 + half * 8 + 8, :] = jnp.where(lane == 127, counts, c) if half else c
+        pv[half * 8:half * 8 + 8, :] = s
+        pv[16 + half * 8:16 + half * 8 + 8, :] = jnp.where(lane == 127, counts, c) if half else c
+
+    fill.append(pltpu.make_async_copy(pv, pi_ref, smsem.at[4]))
+    fill[4].start()
 
     p_onward(1, 0)
     p_onward(1, 1)
@@ -282,11 +289,11 @@
 
     for ch in range(CHUNKS):
         c_onward(4, ch)
+    p_onward(3, 0)
+    p_onward(3, 1)
     for copy in fill:
         copy.wait()
     c_landed()
-    p_onward(3, 0)
-    p_onward(3, 1)
 
     events = {16: [functools.partial(p_onward, 4, ch) for ch in range(CHUNKS)]}
 
@@ -319,18 +326,13 @@
 
 
 def list_kernel(
-    g_ref, f_ref, acc_ref, pg_ref, ci_ref, pi_ref, pt_ref,
+    g_ref, f_ref, acc_ref, pg_ref, ci, pi, pt_ref,
     child_out, pattern_out, incoming_out,
-    ci, pi, child, incoming, sem,
+    child, incoming, sums, sem,
 ):
     r = lax.axis_index("clus")
-    fill_p = pltpu.make_async_copy(pi_ref, pi, sem.at[0])
-    fill_c = pltpu.make_async_copy(ci_ref, ci, sem.at[1])
-    fill_p.start()
-    fill_c.start()
     pattern = pltpu.make_async_copy(pg_ref.at[rows_at(r * 128, 128), :], pattern_out, sem.at[2])
     pattern.start()
-    fill_p.wait()
 
     def run(count, width, last, chunk, total, start=0):
         if start >= last:
@@ -366,7 +368,6 @@
     lax.fori_loop(0, 4, parent, 0)
     done = pltpu.make_async_copy(incoming, incoming_out, sem.at[3])
     done.start()
-    fill_c.wait()
 
     def tail(p, carry):
         def chunk(start, stop, total):
@@ -381,16 +382,24 @@
 
         start = (acc_ref[rows_at(p * 16, 8), :], acc_ref[rows_at(p * 16 + 8, 8), :])
         one, two = run(ci[32 + p, 127] - HEAD, CHILD_TAIL, SLOTS - HEAD, chunk, start)
-        child[p, 0] = (one - pltpu.roll(one, 64, 1))[:, :64]
-        child[p, 1] = (two + pltpu.roll(two, 64, 1))[:, :64]
+        sums[0, p] = one
+        sums[1, p] = two
         return carry
 
-    lax.fori_loop(0, 32, tail, 0)
-    last = pltpu.make_async_copy(child, child_out, sem.at[4])
-    last.start()
+    parts = []
+    for i in range(4):
+        lax.fori_loop(8 * i, 8 * i + 8, tail, 0)
+        group = pl.ds(8 * i, 8)
+        one, two = sums[0, group].reshape(64, 128), sums[1, group].reshape(64, 128)
+        re, im = one - pltpu.roll(one, 64, 1), two + pltpu.roll(two, 64, 1)
+        child[group, 0] = re[:, :64].reshape(8, 8, 64)
+        child[group, 1] = im[:, :64].reshape(8, 8, 64)
+        parts.append(pltpu.make_async_copy(child.at[group], child_out.at[group], sem.at[4 + i]))
+        parts[i].start()
     pattern.wait()
     done.wait()
-    last.wait()
+    for part in parts:
+        part.wait()
 
 
 def local(
@@ -409,11 +418,11 @@
             jax.ShapeDtypeStruct((6144, 128), f32),
             jax.ShapeDtypeStruct((512, 128), f32),
             jax.ShapeDtypeStruct((2080, 128), f32),
-            jax.ShapeDtypeStruct((64, 128), i32),
-            jax.ShapeDtypeStruct((32, 128), i32),
+            pltpu.SMEM((64, 128), i32),
+            pltpu.SMEM((32, 128), i32),
         ),
         in_specs=[hbm] * 13,
-        out_specs=(vmem,) * 6,
+        out_specs=(vmem,) * 4 + (pl.BlockSpec(memory_space=pltpu.SMEM),) * 2,
         scratch_shapes=[
             pltpu.VMEM((32, 2, 8, 64), f32),
             pltpu.VMEM((SLOTS, 128), i32),
@@ -434,11 +443,12 @@
             pltpu.VMEM((512, 128), f32),
             pltpu.VMEM((128, 256), f32),
             pltpu.VMEM((2, 128, 128), f32),
+            pltpu.VMEM((32, 128), i32),
             pltpu.VMEM((4, 128, 128), i32),
             pltpu.SMEM((32, 128), i32),
             pltpu.SMEM((32, 128), i32),
             dma((13,)),
-            dma((2,)),
+            dma((5,)),
             dma((2,)),
             dma((2,)),
             dma((2, 4, CHUNKS)),
@@ -477,14 +487,13 @@
             jax.ShapeDtypeStruct((128, 128), f32),
             jax.ShapeDtypeStruct((128, 128), f32),
         ),
-        in_specs=[vmem] * 7,
+        in_specs=[vmem] * 4 + [pl.BlockSpec(memory_space=pltpu.SMEM)] * 2 + [vmem],
         out_specs=(hbm, hbm, hbm),
         scratch_shapes=[
-            pltpu.SMEM((64, 128), i32),
-            pltpu.SMEM((32, 128), i32),
             pltpu.VMEM((32, 2, 8, 64), f32),
             pltpu.VMEM((128, 128), f32),
-            dma((5,)),
+            pltpu.VMEM((2, 32, 8, 128), f32),
+            dma((8,)),
         ],
         compiler_params=pltpu.CompilerParams(vmem_limit_bytes=24 * 2**20),
         name="lists",

time: 41.6 us -> 40 us (0.962)
  the two profiles are of different devices: /device:TPU:1 before, /device:TPU:97 now
where the time goes in v4:
time: 40 us; the launch traced here: 39.9 us
  Pallas kernels  39.2 us (98%)
  between operations  0.68 us (2%)
    pallas_call x1, Pallas kernels, local(): pl.pallas_call(gather_kernel, out_shape=(jax.ShapeDtypeStruct((4096, 128)...  32.8 us
    pallas_call x1, Pallas kernels, local(): pl.pallas_call(list_kernel, out_shape=(jax.ShapeDtypeStruct((32, 2, 8, 64...  6.38 us

profile of v4, /device:TPU:97, one launch (start us, length us, event | category | flops | bytes accessed | tf_op | source)
XLA Modules:
  0.0 39.9 jit_solution(11639921178018911863)
XLA Ops:
  0.6 0.0 slice-start
  0.6 0.0 slice-start.1
  0.7 32.8 %gather.1 = (f32[4096,128]{1,0:T(8,128)S(1)}, f32[6144,128]{1,0:T(8,128)S(1)}, f32[512,128]{1,0:T(8,128)S(1)}, f32[2080,128]{1,0:T(8,128)S(1)}, s32[64,128]{1,0:T(8,128)S(4)}, /*index=5*/s32[32,128]{1,0:T(8,128)S(4)}) custom-call(f32[32,2,8,64]{3,2,1,0:T(8,128)} %pat_hbm.1, s32[189,512]{1,0:T(8,128)} %bitcast.16, s32[189,512]{1,0:T(8,128)} %bitcast.17, ...), custom_call_target="tpu_custom_call" | custom-call | flops 30000001024 | bytes 8000000 | tf_op jit(solution)/shard_map/gather/pallas_call | solution.py:414
  33.5 0.0 slice-done
  33.5 0.0 slice-done.1
  33.5 6.4 %lists.1 = (f32[32,2,8,64]{3,2,1,0:T(8,128)}, f32[128,128]{1,0:T(8,128)}, f32[128,128]{1,0:T(8,128)}) custom-call(f32[4096,128]{1,0:T(8,128)S(1)} %get-tuple-element.12.g_ref, f32[6144,128]{1,0:T(8,128)S(1)} %get-tuple-element.13.f_ref, f32[512,128]{1,0:T(8,128)S(1)} %get-tuple-element.14.acc_ref, f32[2080,128]{1,0:T(8,128)S(1)} %get-tuple-element.15.pg_ref, ...), custom_call_target="tpu_custom_call" | custom-call | tf_op jit(solution)/shard_map/lists/pallas_call | solution.py:483
  (1 shorter events, 0.0 us)
Async XLA Ops:
  0.6 32.8 %slice-start = ((s8[5177344]{0:T(1024)(128)(4,1)}), s8[4194304]{0:T(1024)(128)(4,1)S(1)}, s32[]{:S(2)}) async-start(s8[5177344]{0:T(1024)(128)(4,1)} %bitcast.12), calls=%async_computation | async-start | bytes 8388608
  0.6 32.8 %slice-start.1 = ((s8[5177344]{0:T(1024)(128)(4,1)}), s8[983040]{0:T(1024)(128)(4,1)S(1)}, s32[]{:S(2)}) async-start(s8[5177344]{0:T(1024)(128)(4,1)} %bitcast.12), calls=%async_computation.1 | async-start | bytes 1966080

commit v5 on v4

--- a/solution.py
+++ b/solution.py
@@ -10,7 +10,7 @@
 MESH = pl.DeviceIdType.MESH
 SLOTS = 189
 CLASSES = 316
-HEAD = 64
+HEAD = 32
 CHILD_TAIL = 25
 PARENT_TAIL = 27
 CHUNKS = 2
@@ -26,13 +26,19 @@
     g_ref, f_ref, acc_ref, pg_ref, ci_ref, pi_ref,
     pat, sv, cv, ccnt, psv, pcv, pcnt, tab, thi, thw, phi, phw, ang,
     own, hs, hr, zs, pair, turns, pv, ta, sa_s, sa_c,
-    loc, smsem, hsend, hrecv, csend, crecv, cssend, csrecv, psend, precv, pssend, psrecv,
+    loc, smsem, hsend, hrecv, csend, crecv, cssend, csrecv, psend, precv,
 ):
     r = lax.axis_index("clus")
     a = lax.axis_index("ang")
     sib = r + 1 - 2 * lax.rem(r, 2)
     up, down = lax.rem(r + 2, 16), lax.rem(r + 14, 16)
     ahead, behind = lax.rem(a + 1, 16), lax.rem(a + 15, 16)
+
+    barrier = pltpu.get_barrier_semaphore()
+    for target in (up, down, sib):
+        pl.semaphore_signal(barrier, inc=1, device_id={"clus": target}, device_id_type=MESH)
+    for target in (ahead, behind):
+        pl.semaphore_signal(barrier, inc=1, device_id={"ang": target}, device_id_type=MESH)
 
     lane_block = pl.ds(pl.multiple_of(lax.div(r, 4) * 128, 128), 128)
     row_block = rows_at(lax.div(r, 2) * 8, 8)
@@ -55,11 +61,6 @@
     for copy in copies:
         copy.start()
 
-    barrier = pltpu.get_barrier_semaphore()
-    for target in (up, down, sib):
-        pl.semaphore_signal(barrier, inc=1, device_id={"clus": target}, device_id_type=MESH)
-    for target in (ahead, behind):
-        pl.semaphore_signal(barrier, inc=1, device_id={"ang": target}, device_id_type=MESH)
     pl.semaphore_wait(barrier, 5)
 
     def mover(buffer, block_rows, send, recv, sib_send, sib_recv):
@@ -111,24 +112,23 @@
                         ring(way, step + 1, ch).start()
                     side((8 - step) if way == 0 else step, ch).start()
 
-        def landed():
-            for k in range(8):
+        def landed(places):
+            for k in places:
                 for ch in range(CHUNKS):
                     side(k, ch, mine=False).wait_recv()
 
-        def drained():
+        def drained(steps, places):
             for ch in range(CHUNKS):
-                for step in range(1, 5):
+                for step in steps:
                     for way in (0, 1):
                         if uses(way, step, ch):
                             ring(way, step, ch).wait_send()
-                for k in range(8):
+                for k in places:
                     side(k, ch).wait_send()
 
         return first, onward, landed, drained
 
     c_first, c_onward, c_landed, c_drained = mover(g_ref, 256, csend, crecv, cssend, csrecv)
-    p_first, p_onward, p_landed, p_drained = mover(pg_ref, 128, psend, precv, pssend, psrecv)
 
     copies[0].wait()
     size = 32 // CHUNKS
@@ -139,16 +139,31 @@
         g_ref[rows_at(r * 256 + ch * size * 8, size * 8), :] = x
         c_first(ch)
 
-    halo = []
-    for way in (0, 1):
-        for j in range(2):
-            hs[way, j * 32:(j + 1) * 32, :] = own[pl.ds((6 if way == 0 else 0) + j, 32, stride=8), :]
-        copy = pltpu.make_async_remote_copy(
-            src_ref=hs.at[way], dst_ref=hr.at[way], send_sem=hsend.at[way], recv_sem=hrecv.at[way],
+    def edge(k, way):
+        return pltpu.make_async_remote_copy(
+            src_ref=hs.at[k, way], dst_ref=hr.at[k, way], send_sem=hsend.at[k, way], recv_sem=hrecv.at[k, way],
             device_id={"ang": ahead if way == 0 else behind}, device_id_type=MESH,
         )
-        copy.start()
-        halo.append(copy)
+
+    def owner(k):
+        return lax.rem(r + 2 * k, 16)
+
+    def edges(k):
+        own[...] = g_ref[rows_at(owner(k) * 256, 256), :]
+        for way in (0, 1):
+            for j in range(2):
+                hs[k, way, j * 32:(j + 1) * 32, :] = own[pl.ds((6 if way == 0 else 0) + j, 32, stride=8), :]
+            edge(k, way).start()
+
+    def aside(k, mine=True):
+        block = pg_ref.at[rows_at(lax.rem((r if mine else sib) + 2 * k, 16) * 128, 128), :]
+        return pltpu.make_async_remote_copy(
+            src_ref=block, dst_ref=block, send_sem=psend.at[k], recv_sem=precv.at[k],
+            device_id={"clus": sib}, device_id_type=MESH,
+        )
+
+    edges(0)
+
 
     for i in (7, 8, 9, 10, 11):
         copies[i].wait()
@@ -173,33 +188,39 @@
             tap = tap + jnp.where(offset[i:i + 1, :] == base + d, weights[i:i + 1, :], 0.0)
         taps.append(tap)
 
-    for copy in halo:
-        copy.wait_recv()
-    cols = [hr[0, :32, :], hr[0, 32:, :]]
-    cols += [own[pl.ds(j, 32, stride=8), :] for j in range(8)]
-    cols += [hr[1, :32, :], hr[1, 32:, :]]
-    for j in range(16):
-        z = jnp.zeros((32, 128), jnp.float32)
-        for d in range(5):
-            z = z + taps[d][:, j:j + 1] * cols[j // 2 + d]
-        zs[pl.ds(j, 32, stride=16), :] = z
-
-    for parent in range(4):
-        y = jnp.dot(
-            zs[parent * 128:(parent + 1) * 128, :], pair[...],
-            precision=lax.Precision.HIGHEST, preferred_element_type=jnp.float32,
-        )
-        re = y[:, :128] * turns[0] - y[:, 128:] * turns[1]
-        im = y[:, :128] * turns[1] + y[:, 128:] * turns[0]
-        re = jnp.sum(re.reshape(8, 16, 128), axis=0)
-        im = jnp.sum(im.reshape(8, 16, 128), axis=0)
-        pg_ref[rows_at(r * 128 + parent * 32, 16), :] = re
-        pg_ref[rows_at(r * 128 + parent * 32 + 16, 16), :] = im
-        if parent == 1:
-            c_onward(1, 0)
-            c_onward(1, 1)
-            p_first(0)
-    p_first(1)
+    def aggregate(k):
+        for way in (0, 1):
+            edge(k, way).wait_recv()
+        own[...] = g_ref[rows_at(owner(k) * 256, 256), :]
+        cols = [hr[k, 0, :32, :], hr[k, 0, 32:, :]]
+        cols += [own[pl.ds(j, 32, stride=8), :] for j in range(8)]
+        cols += [hr[k, 1, :32, :], hr[k, 1, 32:, :]]
+        for j in range(16):
+            z = jnp.zeros((32, 128), jnp.float32)
+            for d in range(5):
+                z = z + taps[d][:, j:j + 1] * cols[j // 2 + d]
+            zs[pl.ds(j, 32, stride=16), :] = z
+        for parent in range(4):
+            y = jnp.dot(
+                zs[parent * 128:(parent + 1) * 128, :], pair[...],
+                precision=lax.Precision.HIGHEST, preferred_element_type=jnp.float32,
+            )
+            re = y[:, :128] * turns[0] - y[:, 128:] * turns[1]
+            im = y[:, :128] * turns[1] + y[:, 128:] * turns[0]
+            re = jnp.sum(re.reshape(8, 16, 128), axis=0)
+            im = jnp.sum(im.reshape(8, 16, 128), axis=0)
+            at = owner(k) * 128 + parent * 32
+            pg_ref[rows_at(at, 16), :] = re
+            pg_ref[rows_at(at + 16, 16), :] = im
+        aside(k).start()
+
+    def pair_of(step):
+        def one(i, carry):
+            aggregate(8 - step + i * (2 * step - 8))
+            return carry
+
+        lax.fori_loop(0, 2, one, 0)
+
     pg_ref[2048:2080, :] = jnp.zeros((32, 128), jnp.float32)
 
     for i in (1, 2, 3):
@@ -223,22 +244,29 @@
     for copy in fill:
         copy.start()
 
-    s, c = lists(HEAD, SLOTS)
-    rest = 128 - (SLOTS - HEAD)
-    s = jnp.concatenate([s * 8, jnp.zeros((rest, 128), jnp.int32)], axis=0)
-    c = jnp.concatenate([c * 16, jnp.full((rest, 128), CLASSES * 16, jnp.int32)], axis=0)
-    c = jnp.where(slot == 127, count_row, c)
-    ta[2] = s.T
-    ta[3] = c.T
-    fill += [
-        pltpu.make_async_copy(ta.at[2, own_rows, :], ci_ref.at[:32, :], smsem.at[2]),
-        pltpu.make_async_copy(ta.at[3, own_rows, :], ci_ref.at[32:, :], smsem.at[3]),
-    ]
-    fill[2].start()
-    fill[3].start()
-
-    c_onward(2, 0)
-    c_onward(2, 1)
+    for half, (begin, end) in enumerate(((HEAD, HEAD + 128), (HEAD + 128, SLOTS))):
+        s, c = lists(begin, end)
+        s, c = s * 8, c * 16
+        if half:
+            rest = 128 - (end - begin)
+            s = jnp.concatenate([s, jnp.zeros((rest, 128), jnp.int32)], axis=0)
+            c = jnp.concatenate([c, jnp.full((rest, 128), CLASSES * 16, jnp.int32)], axis=0)
+            c = jnp.where(slot == 127, count_row, c)
+        ta[2 + half] = s.T
+        ta[4 + half] = c.T
+    for i in range(4):
+        fill.append(
+            pltpu.make_async_copy(ta.at[2 + i, own_rows, :], ci_ref.at[pl.ds(32 * i, 32), :], smsem.at[2 + i])
+        )
+        fill[2 + i].start()
+
+
+    c_onward(1, 0)
+    c_onward(1, 1)
+    edges(7)
+    edges(1)
+
+    aggregate(0)
 
     for i in (4, 5, 6):
         copies[i].wait()
@@ -260,11 +288,9 @@
         pv[half * 8:half * 8 + 8, :] = s
         pv[16 + half * 8:16 + half * 8 + 8, :] = jnp.where(lane == 127, counts, c) if half else c
 
-    fill.append(pltpu.make_async_copy(pv, pi_ref, smsem.at[4]))
-    fill[4].start()
-
-    p_onward(1, 0)
-    p_onward(1, 1)
+    fill.append(pltpu.make_async_copy(pv, pi_ref, smsem.at[6]))
+    fill[6].start()
+
 
     copies[12].wait()
 
@@ -278,24 +304,39 @@
             f_ref[pl.ds(lo * 16 + col, 128, stride=16), :] = y
             f_ref[pl.ds(lo * 16 + col + 8, 128, stride=16), :] = pltpu.roll(y, 64, 1)
 
+
     for col in range(4):
         operators(col)
+
+    c_onward(2, 0)
+    c_onward(2, 1)
+    edges(6)
+    edges(2)
+
+    pair_of(1)
+
+    for col in range(4, 8):
+        operators(col)
+
     c_onward(3, 0)
     c_onward(3, 1)
-    for col in range(4, 8):
-        operators(col)
-    p_onward(2, 0)
-    p_onward(2, 1)
-
-    for ch in range(CHUNKS):
-        c_onward(4, ch)
-    p_onward(3, 0)
-    p_onward(3, 1)
+    edges(5)
+    edges(3)
+
+    pair_of(2)
+
+    c_drained((1, 2), (0, 7, 1, 6, 2))
+    c_landed((0, 7, 1, 6, 2))
     for copy in fill:
         copy.wait()
-    c_landed()
-
-    events = {16: [functools.partial(p_onward, 4, ch) for ch in range(CHUNKS)]}
+
+    c_onward(4, 0)
+    c_onward(4, 1)
+    edges(4)
+
+    pair_of(3)
+
+    c_landed((5, 3, 4))
 
     g3, f4 = g_ref.reshape(512, 8, 128), f_ref.reshape(384, 2, 8, 128)
 
@@ -309,20 +350,21 @@
             two = two + x * f4[c, 1]
         acc_ref[rows_at(p * 16, 8), :] = one
         acc_ref[rows_at(p * 16 + 8, 8), :] = two
-        for at, todo in events.items():
-            @pl.when(p == at)
-            def _():
-                for go in todo:
-                    go()
+
+        @pl.when(p == 4)
+        def _():
+            aggregate(4)
+
         return carry
 
     lax.fori_loop(0, 32, head, 0)
 
-    p_landed()
-    for copy in halo:
-        copy.wait_send()
-    c_drained()
-    p_drained()
+    c_drained((3, 4), (5, 3, 4))
+    for k in range(8):
+        for way in (0, 1):
+            edge(k, way).wait_send()
+        aside(k, mine=False).wait_recv()
+        aside(k).wait_send()
 
 
 def list_kernel(
@@ -373,15 +415,16 @@
         def chunk(start, stop, total):
             one, two = total
             for m in range(start, stop):
-                s = pl.multiple_of(ci[p, m], 8)
-                c = pl.multiple_of(ci[32 + p, m], 16)
+                row = p + 32 * (m // 128)
+                s = pl.multiple_of(ci[row, m % 128], 8)
+                c = pl.multiple_of(ci[64 + row, m % 128], 16)
                 x = g_ref[pl.ds(s, 8), :]
                 one = one + x * f_ref[pl.ds(c, 8), :]
                 two = two + x * f_ref[pl.ds(c + 8, 8), :]
             return one, two
 
         start = (acc_ref[rows_at(p * 16, 8), :], acc_ref[rows_at(p * 16 + 8, 8), :])
-        one, two = run(ci[32 + p, 127] - HEAD, CHILD_TAIL, SLOTS - HEAD, chunk, start)
+        one, two = run(ci[96 + p, 127] - HEAD, CHILD_TAIL, SLOTS - HEAD, chunk, start)
         sums[0, p] = one
         sums[1, p] = two
         return carry
@@ -418,7 +461,7 @@
             jax.ShapeDtypeStruct((6144, 128), f32),
             jax.ShapeDtypeStruct((512, 128), f32),
             jax.ShapeDtypeStruct((2080, 128), f32),
-            pltpu.SMEM((64, 128), i32),
+            pltpu.SMEM((128, 128), i32),
             pltpu.SMEM((32, 128), i32),
         ),
         in_specs=[hbm] * 13,
@@ -438,27 +481,25 @@
             pltpu.VMEM((4, 16), f32),
             pltpu.VMEM((128, 128), f32),
             pltpu.VMEM((256, 128), f32),
-            pltpu.VMEM((2, 64, 128), f32),
-            pltpu.VMEM((2, 64, 128), f32),
+            pltpu.VMEM((8, 2, 64, 128), f32),
+            pltpu.VMEM((8, 2, 64, 128), f32),
             pltpu.VMEM((512, 128), f32),
             pltpu.VMEM((128, 256), f32),
             pltpu.VMEM((2, 128, 128), f32),
             pltpu.VMEM((32, 128), i32),
-            pltpu.VMEM((4, 128, 128), i32),
+            pltpu.VMEM((6, 128, 128), i32),
             pltpu.SMEM((32, 128), i32),
             pltpu.SMEM((32, 128), i32),
             dma((13,)),
-            dma((5,)),
-            dma((2,)),
-            dma((2,)),
+            dma((7,)),
+            dma((8, 2)),
+            dma((8, 2)),
             dma((2, 4, CHUNKS)),
             dma((8, CHUNKS)),
             dma((8, CHUNKS)),
             dma((8, CHUNKS)),
-            dma((2, 4, CHUNKS)),
-            dma((8, CHUNKS)),
-            dma((8, CHUNKS)),
-            dma((8, CHUNKS)),
+            dma((8,)),
+            dma((8,)),
         ],
         compiler_params=pltpu.CompilerParams(
             collective_id=0, has_side_effects=True, vmem_limit_bytes=24 * 2**20

time: 40 us -> 39.6 us (0.990)
  the two profiles are of different devices: /device:TPU:97 before, /device:TPU:1 now
where the time goes in v5:
time: 39.6 us
  Pallas kernels  38.9 us (98%)
  between operations  0.68 us (2%)
    pallas_call x1, Pallas kernels, local(): pl.pallas_call(gather_kernel, out_shape=(jax.ShapeDtypeStruct((4096, 128)...  33.5 us
    pallas_call x1, Pallas kernels, local(): pl.pallas_call(list_kernel, out_shape=(jax.ShapeDtypeStruct((32, 2, 8, 64...  5.31 us

profile of v5, /device:TPU:1, one launch (start us, length us, event | category | flops | bytes accessed | tf_op | source)
XLA Modules:
  0.0 39.6 jit_solution(15318526940574820254)
XLA Ops:
  0.6 0.0 slice-start
  0.6 0.0 slice-start.1
  0.7 33.5 %gather.1 = (f32[4096,128]{1,0:T(8,128)S(1)}, f32[6144,128]{1,0:T(8,128)S(1)}, f32[512,128]{1,0:T(8,128)S(1)}, f32[2080,128]{1,0:T(8,128)S(1)}, s32[128,128]{1,0:T(8,128)S(4)}, /*index=5*/s32[32,128]{1,0:T(8,128)S(4)}) custom-call(f32[32,2,8,64]{3,2,1,0:T(8,128)} %pat_hbm.1, s32[189,512]{1,0:T(8,128)} %bitcast.16, s32[189,512]{1,0:T(8,128)} %bitcast.17, ...), custom_call_target="tpu_custom_call" | custom-call | flops 30000001024 | bytes 8000000 | tf_op jit(solution)/shard_map/gather/pallas_call | solution.py:457
  34.2 0.0 slice-done
  34.2 0.0 slice-done.1
  34.2 5.3 %lists.1 = (f32[32,2,8,64]{3,2,1,0:T(8,128)}, f32[128,128]{1,0:T(8,128)}, f32[128,128]{1,0:T(8,128)}) custom-call(f32[4096,128]{1,0:T(8,128)S(1)} %get-tuple-element.12.g_ref, f32[6144,128]{1,0:T(8,128)S(1)} %get-tuple-element.13.f_ref, f32[512,128]{1,0:T(8,128)S(1)} %get-tuple-element.14.acc_ref, f32[2080,128]{1,0:T(8,128)S(1)} %get-tuple-element.15.pg_ref, ...), custom_call_target="tpu_custom_call" | custom-call | tf_op jit(solution)/shard_map/lists/pallas_call | solution.py:524
  (1 shorter events, 0.0 us)
Async XLA Ops:
  0.6 33.6 %slice-start = ((s8[5177344]{0:T(1024)(128)(4,1)}), s8[4194304]{0:T(1024)(128)(4,1)S(1)}, s32[]{:S(2)}) async-start(s8[5177344]{0:T(1024)(128)(4,1)} %bitcast.12), calls=%async_computation | async-start | bytes 8388608
  0.6 33.6 %slice-start.1 = ((s8[5177344]{0:T(1024)(128)(4,1)}), s8[983040]{0:T(1024)(128)(4,1)S(1)}, s32[]{:S(2)}) async-start(s8[5177344]{0:T(1024)(128)(4,1)} %bitcast.12), calls=%async_computation.1 | async-start | bytes 1966080

commit v6 on v5

--- a/solution.py
+++ b/solution.py
@@ -10,8 +10,8 @@
 MESH = pl.DeviceIdType.MESH
 SLOTS = 189
 CLASSES = 316
-HEAD = 32
-CHILD_TAIL = 25
+HEAD = 52
+CHILD_TAIL = 35
 PARENT_TAIL = 27
 CHUNKS = 2
 
@@ -25,7 +25,7 @@
     thi_hbm, thw_hbm, phi_hbm, phw_hbm, ang_hbm,
     g_ref, f_ref, acc_ref, pg_ref, ci_ref, pi_ref,
     pat, sv, cv, ccnt, psv, pcv, pcnt, tab, thi, thw, phi, phw, ang,
-    own, hs, hr, zs, pair, turns, pv, ta, sa_s, sa_c,
+    own, hs, hr, zs, pair, turns, spread, pv, ta, sa_s, sa_c,
     loc, smsem, hsend, hrecv, csend, crecv, cssend, csrecv, psend, precv,
 ):
     r = lax.axis_index("clus")
@@ -188,6 +188,10 @@
             tap = tap + jnp.where(offset[i:i + 1, :] == base + d, weights[i:i + 1, :], 0.0)
         taps.append(tap)
 
+    for j in range(16):
+        for d in range(5):
+            spread[5 * j + d] = jnp.broadcast_to(taps[d][:, j:j + 1], (8, 128))
+
     def aggregate(k):
         for way in (0, 1):
             edge(k, way).wait_recv()
@@ -195,11 +199,12 @@
         cols = [hr[k, 0, :32, :], hr[k, 0, 32:, :]]
         cols += [own[pl.ds(j, 32, stride=8), :] for j in range(8)]
         cols += [hr[k, 1, :32, :], hr[k, 1, 32:, :]]
+        cols = [x.reshape(4, 8, 128) for x in cols]
         for j in range(16):
-            z = jnp.zeros((32, 128), jnp.float32)
-            for d in range(5):
-                z = z + taps[d][:, j:j + 1] * cols[j // 2 + d]
-            zs[pl.ds(j, 32, stride=16), :] = z
+            z = cols[j // 2] * spread[5 * j]
+            for d in range(1, 5):
+                z = z + cols[j // 2 + d] * spread[5 * j + d]
+            zs[pl.ds(j, 32, stride=16), :] = z.reshape(32, 128)
         for parent in range(4):
             y = jnp.dot(
                 zs[parent * 128:(parent + 1) * 128, :], pair[...],
@@ -486,6 +491,7 @@
             pltpu.VMEM((512, 128), f32),
             pltpu.VMEM((128, 256), f32),
             pltpu.VMEM((2, 128, 128), f32),
+            pltpu.VMEM((80, 8, 128), f32),
             pltpu.VMEM((32, 128), i32),
             pltpu.VMEM((6, 128, 128), i32),
             pltpu.SMEM((32, 128), i32),

time: 39.6 us -> 39.2 us (0.990)
  Pallas kernels: 38.9 us -> 38.1 us
    pallas_call x1, Pallas kernels: 5.31 us -> 4.54 us  [local(): pl.pallas_call(list_kernel, out_shape=(jax.ShapeDtypeStruct((32, 2, 8, 64...]
where the time goes in v6:
time: 39.2 us; the launch traced here: 38.8 us
  Pallas kernels  38.1 us (97%)
  between operations  0.68 us (2%)
    pallas_call x1, Pallas kernels, local(): pl.pallas_call(gather_kernel, out_shape=(jax.ShapeDtypeStruct((4096, 128)...  33.6 us
    pallas_call x1, Pallas kernels, local(): pl.pallas_call(list_kernel, out_shape=(jax.ShapeDtypeStruct((32, 2, 8, 64...  4.54 us

profile of v6, /device:TPU:1, one launch (start us, length us, event | category | flops | bytes accessed | tf_op | source)
XLA Modules:
  0.0 38.8 jit_solution(17295487586672202926)
XLA Ops:
  0.6 0.0 slice-start
  0.6 0.0 slice-start.1
  0.7 33.6 %gather.1 = (f32[4096,128]{1,0:T(8,128)S(1)}, f32[6144,128]{1,0:T(8,128)S(1)}, f32[512,128]{1,0:T(8,128)S(1)}, f32[2080,128]{1,0:T(8,128)S(1)}, s32[128,128]{1,0:T(8,128)S(4)}, /*index=5*/s32[32,128]{1,0:T(8,128)S(4)}) custom-call(f32[32,2,8,64]{3,2,1,0:T(8,128)} %pat_hbm.1, s32[189,512]{1,0:T(8,128)} %bitcast.16, s32[189,512]{1,0:T(8,128)} %bitcast.17, ...), custom_call_target="tpu_custom_call" | custom-call | flops 30000001024 | bytes 8000000 | tf_op jit(solution)/shard_map/gather/pallas_call | solution.py:462
  34.2 0.0 slice-done
  34.2 0.0 slice-done.1
  34.3 4.5 %lists.1 = (f32[32,2,8,64]{3,2,1,0:T(8,128)}, f32[128,128]{1,0:T(8,128)}, f32[128,128]{1,0:T(8,128)}) custom-call(f32[4096,128]{1,0:T(8,128)S(1)} %get-tuple-element.12.g_ref, f32[6144,128]{1,0:T(8,128)S(1)} %get-tuple-element.13.f_ref, f32[512,128]{1,0:T(8,128)S(1)} %get-tuple-element.14.acc_ref, f32[2080,128]{1,0:T(8,128)S(1)} %get-tuple-element.15.pg_ref, ...), custom_call_target="tpu_custom_call" | custom-call | tf_op jit(solution)/shard_map/lists/pallas_call | solution.py:530
  (1 shorter events, 0.0 us)
Async XLA Ops:
  0.6 33.6 %slice-start = ((s8[5177344]{0:T(1024)(128)(4,1)}), s8[4194304]{0:T(1024)(128)(4,1)S(1)}, s32[]{:S(2)}) async-start(s8[5177344]{0:T(1024)(128)(4,1)} %bitcast.12), calls=%async_computation | async-start | bytes 8388608
  0.6 33.6 %slice-start.1 = ((s8[5177344]{0:T(1024)(128)(4,1)}), s8[983040]{0:T(1024)(128)(4,1)S(1)}, s32[]{:S(2)}) async-start(s8[5177344]{0:T(1024)(128)(4,1)} %bitcast.12), calls=%async_computation.1 | async-start | bytes 1966080

commit v7 on v6

--- a/solution.py
+++ b/solution.py
@@ -356,7 +356,7 @@
         acc_ref[rows_at(p * 16, 8), :] = one
         acc_ref[rows_at(p * 16 + 8, 8), :] = two
 
-        @pl.when(p == 4)
+        @pl.when(p == 20)
         def _():
             aggregate(4)
 

time: 39.2 us -> 38.7 us (0.987)
  Pallas kernels: 38.1 us -> 37.2 us
    pallas_call x1, Pallas kernels: 4.54 us -> 3.6 us  [local(): pl.pallas_call(list_kernel, out_shape=(jax.ShapeDtypeStruct((32, 2, 8, 64...]
where the time goes in v7:
time: 38.7 us; the launch traced here: 37.9 us
  Pallas kernels  37.2 us (96%)
  between operations  0.68 us (2%)
    pallas_call x1, Pallas kernels, local(): pl.pallas_call(gather_kernel, out_shape=(jax.ShapeDtypeStruct((4096, 128)...  33.6 us
    pallas_call x1, Pallas kernels, local(): pl.pallas_call(list_kernel, out_shape=(jax.ShapeDtypeStruct((32, 2, 8, 64...  3.6 us

profile of v7, /device:TPU:1, one launch (start us, length us, event | category | flops | bytes accessed | tf_op | source)
XLA Modules:
  0.0 37.9 jit_solution(6607702067301277555)
XLA Ops:
  0.6 0.0 slice-start
  0.6 0.0 slice-start.1
  0.7 33.6 %gather.1 = (f32[4096,128]{1,0:T(8,128)S(1)}, f32[6144,128]{1,0:T(8,128)S(1)}, f32[512,128]{1,0:T(8,128)S(1)}, f32[2080,128]{1,0:T(8,128)S(1)}, s32[128,128]{1,0:T(8,128)S(4)}, /*index=5*/s32[32,128]{1,0:T(8,128)S(4)}) custom-call(f32[32,2,8,64]{3,2,1,0:T(8,128)} %pat_hbm.1, s32[189,512]{1,0:T(8,128)} %bitcast.16, s32[189,512]{1,0:T(8,128)} %bitcast.17, ...), custom_call_target="tpu_custom_call" | custom-call | flops 30000001024 | bytes 8000000 | tf_op jit(solution)/shard_map/gather/pallas_call | solution.py:462
  34.3 0.0 slice-done
  34.3 0.0 slice-done.1
  34.3 3.6 %lists.1 = (f32[32,2,8,64]{3,2,1,0:T(8,128)}, f32[128,128]{1,0:T(8,128)}, f32[128,128]{1,0:T(8,128)}) custom-call(f32[4096,128]{1,0:T(8,128)S(1)} %get-tuple-element.12.g_ref, f32[6144,128]{1,0:T(8,128)S(1)} %get-tuple-element.13.f_ref, f32[512,128]{1,0:T(8,128)S(1)} %get-tuple-element.14.acc_ref, f32[2080,128]{1,0:T(8,128)S(1)} %get-tuple-element.15.pg_ref, ...), custom_call_target="tpu_custom_call" | custom-call | tf_op jit(solution)/shard_map/lists/pallas_call | solution.py:530
  (1 shorter events, 0.0 us)
Async XLA Ops:
  0.6 33.7 %slice-start = ((s8[5177344]{0:T(1024)(128)(4,1)}), s8[4194304]{0:T(1024)(128)(4,1)S(1)}, s32[]{:S(2)}) async-start(s8[5177344]{0:T(1024)(128)(4,1)} %bitcast.12), calls=%async_computation | async-start | bytes 8388608
  0.6 33.7 %slice-start.1 = ((s8[5177344]{0:T(1024)(128)(4,1)}), s8[983040]{0:T(1024)(128)(4,1)S(1)}, s32[]{:S(2)}) async-start(s8[5177344]{0:T(1024)(128)(4,1)} %bitcast.12), calls=%async_computation.1 | async-start | bytes 1966080
